TPU v7x, 256 devices: a whole 4x4x8 slice. The times are simulated.
256 devices in a mesh: region: 32 (over z, x), slot: 8 (over y, core).
Axes of the slice: x: 4, y: 4, z: 8, core: 2. Of those that a mesh axis runs over, the one named last changes fastest.
Arguments:
- flux: float32 [8, 1048576], P('slot', 'region'), may hold values from -6 to 6
- prior_flux: float32 [8, 1048576], P('slot', 'region'), may hold values from -6 to 6
- prior_precision: float32 [8, 1048576], P('slot', 'region'), may hold values from 0.2 to 2
- obs_value: float32 [524288], P('region'), may hold values from -10 to 10
- obs_weight: float32 [524288], P('region'), may hold values from 0.25 to 4
- footprint: float32 [8, 32, 32, 8, 4096], P('slot', 'region'), may hold values from -0.25 to 0.25
- counts: int32 [8, 32, 32], P('slot', 'region'), may hold values from 1 to 8, as said below
- obs_blocks: int32 [8, 32, 32, 8], P('slot', 'region'), may hold values from 0 to 255
- cell_blocks: int32 [8, 32, 32, 8], P('slot', 'region'), may hold values from 0 to 511
Outputs:
- increment: float32 [8, 1048576], P('slot', 'region')
- gradient: float32 [8, 1048576], P('slot', 'region')
Inputs may be any that keep to these rules, and one draw needn't show every extreme that they name: `counts`: in every slot some owner region receives 8 live blocks from every source region.
All inputs are finite; a program needn't handle non-finite values.
Results may differ from a plain program's by a relative error of at most 0.00026.
Values sent between devices are 32-bit elements; how exact they have to be, the bound alone decides.
A program may use at most 64 MiB of HBM per device.

v0:
```python
import jax
import jax.numpy as jnp
from jax import lax
from jax.sharding import PartitionSpec as P

BLOCK = 64
ITERS = 2


def body(
    flux,
    prior_flux,
    prior_precision,
    obs_value,
    obs_weight,
    footprint,
    counts,
    obs_blocks,
    cell_blocks,
):
    regions = lax.axis_size("region")
    local_slots = flux.shape[0]
    most = footprint.shape[3]
    cell_count = flux.shape[1] // BLOCK
    obs_count = obs_value.shape[0] // BLOCK
    shape3 = (local_slots, regions, most)
    blocks = footprint.reshape(local_slots, regions, most, BLOCK, BLOCK)
    valid = (
        lax.broadcasted_iota(jnp.int32, shape3, 2) < counts.reshape(local_slots, regions, 1)
    ).astype(jnp.float32)
    targets = obs_blocks.reshape(shape3)
    slot_place = lax.broadcasted_iota(jnp.int32, shape3, 0)
    owner_place = lax.broadcasted_iota(jnp.int32, shape3, 1)
    cell_rows = (slot_place * cell_count + cell_blocks.reshape(shape3)).reshape(-1)
    dense_rows = (owner_place * obs_count + targets).reshape(-1)
    incoming = lax.all_to_all(
        obs_blocks, "region", split_axis=2, concat_axis=1, tiled=True
    ).reshape(-1)

    def forward(field):
        picked = field.reshape(-1, BLOCK)[cell_rows].reshape(local_slots, regions, most, BLOCK)
        part = jnp.einsum("sqkoc,sqkc->sqko", blocks, picked, precision=lax.Precision.HIGHEST)
        part = part * valid[..., None]
        dense = jax.ops.segment_sum(part.reshape(-1, BLOCK), dense_rows, regions * obs_count)
        local = lax.psum_scatter(dense, "region", scatter_dimension=0, tiled=True)
        return lax.psum(local, "slot").reshape(-1)

    state = flux
    increment = jnp.zeros_like(flux)
    gradient = jnp.zeros_like(flux)
    for step in range(ITERS):
        predicted = forward(state)
        weighted = obs_weight * (predicted - obs_value)
        rows = weighted.reshape(obs_count, BLOCK)
        adjoint_picked = rows[incoming].reshape(local_slots, regions, 1, most, BLOCK)
        back = lax.all_to_all(
            adjoint_picked, "region", split_axis=1, concat_axis=2, tiled=True
        ).reshape(local_slots, regions, most, BLOCK)
        term = jnp.einsum("sqkoc,sqko->sqkc", blocks, back, precision=lax.Precision.HIGHEST)
        term = term * valid[..., None]
        summed = jax.ops.segment_sum(term.reshape(-1, BLOCK), cell_rows, local_slots * cell_count)
        gradient = summed.reshape(local_slots, -1) + prior_precision * (state - prior_flux)
        square_sum = jnp.sum(gradient * gradient)
        prior_sum = jnp.sum(prior_precision * gradient * gradient)
        image = forward(gradient)
        sounding_part = jnp.sum(obs_weight * image * image)
        totals = lax.psum((square_sum, prior_sum), ("region", "slot"))
        sounding_total = lax.psum(sounding_part, "region")
        numer = totals[0]
        denom = sounding_total + totals[1]
        alpha = numer / denom
        state = state - alpha * gradient
        increment = increment - alpha * gradient
    return (increment, gradient)


def solution(mesh):
    placed = (
        P("slot", "region"),
        P("slot", "region"),
        P("slot", "region"),
        P("region"),
        P("region"),
        P("slot", "region", None, None, None),
        P("slot", "region", None),
        P("slot", "region", None, None),
        P("slot", "region", None, None),
    )
    return jax.shard_map(
        body,
        mesh=mesh,
        in_specs=placed,
        out_specs=(P("slot", "region"), P("slot", "region")),
        check_vma=False,
    )
```

profile of v0, /device:TPU:1, one launch (start us, length us, event | category | flops | bytes accessed | tf_op | source)
XLA Modules:
  0.0 1600.5 jit_solution(2445277713520551143)
XLA Ops:
  10.4 1.9 reduce.16
  12.3 7.9 reshape.259
  20.9 15.4 fusion.36
  36.4 3.7 scatter_custom_fusion
  40.2 20.2 %all_to_all.12 = s32[1,1,32,8]{3,1,0,2:T(1,128)S(1)} all-to-all(s32[1,1,32,8]{3,1,0,2:T(1,128)S(1)} %copy.18), channel_id=1, replica_groups=mesh['region'=32,'slot'=8] {'region'}, dimensions={2} | all-to-all | bytes 2048 | tf_op jit(solution)/shard_map/all_to_all | solution.py:36
  61.8 198.4 %reduce-scatter.5.cloned.1.call-done = f32[256,64]{1,0:T(8,128)} async-done(((f32[8192,64]{1,0:T(8,128)}), f32[256,64]{1,0:T(8,128)}) %reduce-scatter.5.cloned.1.call-update) | async-done | bytes 65552 | tf_op jit(solution)/shard_map/reduce_scatter | solution.py:45
  260.2 1.6 reshape.261
  261.8 66.6 %all-reduce.7.cloned.1.call-done = f32[16384]{0:T(1024)} async-done(((f32[16384]{0:T(1024)}), f32[16384]{0:T(1024)}) %all-reduce.7.cloned.1.call-update) | async-done | bytes 65552 | tf_op jit(solution)/shard_map/psum | solution.py:46
  330.8 9.5 all-to-all-start.1
  340.7 8.5 all-to-all-done.1
  350.6 9.5 fusion.37
  362.0 2.1 fusion.24
  364.8 15.4 fusion.38
  380.2 3.7 scatter_custom_fusion.2
  384.0 212.1 %reduce-scatter.7.cloned.1.call-done = f32[256,64]{1,0:T(8,128)} async-done(((f32[8192,64]{1,0:T(8,128)}), f32[256,64]{1,0:T(8,128)}) %reduce-scatter.7.cloned.1.call-update) | async-done | bytes 65552 | tf_op jit(solution)/shard_map/reduce_scatter | solution.py:45
  597.8 66.3 %all-reduce.9.cloned.1.call-done = f32[16384]{0:T(1024)} async-done(((f32[16384]{0:T(1024)}), f32[16384]{0:T(1024)}) %all-reduce.9.cloned.1.call-update) | async-done | bytes 65552 | tf_op jit(solution)/shard_map/psum | solution.py:46
  665.6 78.3 %all-reduce.1 = (f32[]{:T(128)}, f32[]{:T(128)}) all-reduce(f32[]{:T(128)} %get-tuple-element.7, f32[]{:T(128)} %get-tuple-element.5), channel_id=1, replica_groups=mesh['region'=32,'slot'=8] {'region','slot'}, use_global_device_ids=true, to_apply=%region_5.0 | all-reduce | flops 2 | bytes 16 | tf_op jit(solution)/shard_map/psum | solution.py:67
  743.9 58.7 %psum.73 = f32[]{:T(128)} all-reduce(f32[]{:T(128)} %fusion.26), channel_id=1, replica_groups=mesh['region'=32,'slot'=8] {'region'}, use_global_device_ids=true, to_apply=%region_10.0 | all-reduce | flops 1 | bytes 8 | tf_op jit(solution)/shard_map/psum | solution.py:68
  805.6 15.4 fusion.39
  820.9 3.7 scatter_custom_fusion.3
  824.7 225.6 %reduce-scatter.9.cloned.1.call-done = f32[256,64]{1,0:T(8,128)} async-done(((f32[8192,64]{1,0:T(8,128)}), f32[256,64]{1,0:T(8,128)}) %reduce-scatter.9.cloned.1.call-update) | async-done | bytes 65552 | tf_op jit(solution)/shard_map/reduce_scatter | solution.py:45
  1052.0 66.4 %all-reduce.11.cloned.1.call-done = f32[16384]{0:T(1024)} async-done(((f32[16384]{0:T(1024)}), f32[16384]{0:T(1024)}) %all-reduce.11.cloned.1.call-update) | async-done | bytes 65552 | tf_op jit(solution)/shard_map/psum | solution.py:46
  1120.2 18.2 %all_to_all.13 = f32[32,1,512]{2,1,0:T(1,128)S(1)} all-to-all(f32[32,1,512]{2,1,0:T(1,128)S(1)} %reshape.446), channel_id=1, replica_groups=mesh['region'=32,'slot'=8] {'region'}, dimensions={0} | all-to-all | bytes 131072 | tf_op jit(solution)/shard_map/all_to_all | solution.py:56
  1139.2 9.5 fusion.40
  1148.7 1.8 scatter_custom_fusion.4
  1150.7 2.1 fusion.25
  1153.6 15.4 fusion.41
  1169.0 3.7 scatter_custom_fusion.5
  1172.8 211.7 %reduce-scatter.11.cloned.1.call-done = f32[256,64]{1,0:T(8,128)} async-done(((f32[8192,64]{1,0:T(8,128)}), f32[256,64]{1,0:T(8,128)}) %reduce-scatter.11.cloned.1.call-update) | async-done | bytes 65552 | tf_op jit(solution)/shard_map/reduce_scatter | solution.py:45
  1386.1 66.5 %all-reduce.13.cloned.1.call-done = f32[16384]{0:T(1024)} async-done(((f32[16384]{0:T(1024)}), f32[16384]{0:T(1024)}) %all-reduce.13.cloned.1.call-update) | async-done | bytes 65552 | tf_op jit(solution)/shard_map/psum | solution.py:46
  1454.0 78.3 %all-reduce = (f32[]{:T(128)}, f32[]{:T(128)}) all-reduce(f32[]{:T(128)} %get-tuple-element.4, f32[]{:T(128)} %get-tuple-element.2), channel_id=1, replica_groups=mesh['region'=32,'slot'=8] {'region','slot'}, use_global_device_ids=true, to_apply=%region_18.0 | all-reduce | flops 2 | bytes 16 | tf_op jit(solution)/shard_map/psum | solution.py:67
  1532.3 58.3 %psum.78 = f32[]{:T(128)} all-reduce(f32[]{:T(128)} %fusion.27), channel_id=1, replica_groups=mesh['region'=32,'slot'=8] {'region'}, use_global_device_ids=true, to_apply=%region_23.0 | all-reduce | flops 1 | bytes 8 | tf_op jit(solution)/shard_map/psum | solution.py:68
  (82 shorter events, 26.0 us)
Async XLA Ops:
  7.2 253.0 %reduce-scatter.5.cloned.1.call-start = ((), (), s32[]{:S(2)}) async-start(), calls=%async_computation.7 | async-start | bytes 4325376 | tf_op jit(solution)/shard_map/reduce_scatter | solution.py:45
  36.3 3.8 copy-start.6
  36.3 292.0 %copy-start.1 = (f32[16384]{0:T(1024)S(1)}, f32[16384]{0:T(1024)}, u32[]{:S(2)}) copy-start(f32[16384]{0:T(1024)} %param.13) | copy-start | bytes 196612
  36.3 292.0 %copy-start.5 = (f32[16384]{0:T(1024)S(1)}, f32[16384]{0:T(1024)}, u32[]{:S(2)}) copy-start(f32[16384]{0:T(1024)} %param.12) | copy-start | bytes 196612
  40.1 288.3 %all-reduce.7.cloned.1.call-start = ((), (), s32[]{:S(2)}) async-start(), calls=%async_computation.8 | async-start | bytes 131072 | tf_op jit(solution)/shard_map/psum | solution.py:46
  330.8 18.4 %all-to-all-start.1 = ((f32[32,1,512]{2,1,0:T(1,128)}), f32[32,1,512]{2,1,0:T(1,128)S(1)}, u32[]{:S(2)}, u32[]{:S(2)}) async-start(f32[32,1,512]{2,1,0:T(1,128)} %reshape.444), calls=%async_computation.2 | async-start | bytes 131072 | tf_op jit(solution)/shard_map/all_to_all | solution.py:56
  340.4 255.7 %reduce-scatter.7.cloned.1.call-start = ((), (), s32[]{:S(2)}) async-start(), calls=%async_computation.9 | async-start | bytes 4325376 | tf_op jit(solution)/shard_map/reduce_scatter | solution.py:45
  350.6 11.3 copy-start
  350.6 11.3 copy-start.3
  350.6 11.3 copy-start.4
  384.0 280.1 %all-reduce.9.cloned.1.call-start = ((), (), s32[]{:S(2)}) async-start(), calls=%async_computation.10 | async-start | bytes 131072 | tf_op jit(solution)/shard_map/psum | solution.py:46
  597.7 452.6 %reduce-scatter.9.cloned.1.call-start = ((), (), s32[]{:S(2)}) async-start(), calls=%async_computation.11 | async-start | bytes 4325376 | tf_op jit(solution)/shard_map/reduce_scatter | solution.py:45
  824.7 293.7 %all-reduce.11.cloned.1.call-start = ((), (), s32[]{:S(2)}) async-start(), calls=%async_computation.12 | async-start | bytes 131072 | tf_op jit(solution)/shard_map/psum | solution.py:46
  1052.0 332.5 %reduce-scatter.11.cloned.1.call-start = ((), (), s32[]{:S(2)}) async-start(), calls=%async_computation.13 | async-start | bytes 4325376 | tf_op jit(solution)/shard_map/reduce_scatter | solution.py:45
  1152.8 439.9 %copy-start.2 = (f32[1,32768]{1,0:T(1,128)}, f32[1,32768]{1,0:T(1,128)S(1)}, u32[]{:S(2)}) copy-start(f32[1,32768]{1,0:T(1,128)S(1)} %get-tuple-element.12) | copy-start | bytes 393220
  1172.7 279.8 %all-reduce.13.cloned.1.call-start = ((), (), s32[]{:S(2)}) async-start(), calls=%async_computation.14 | async-start | bytes 131072 | tf_op jit(solution)/shard_map/psum | solution.py:46
Sparse Core Ops, SparseCore 0:
  40.2 219.8 reduce-scatter.4
  263.1 65.1 all-reduce.6
  384.1 211.9 reduce-scatter.6
  598.9 65.1 all-reduce.8
  824.8 225.4 reduce-scatter.8
  1053.2 65.1 all-reduce.10
  1172.8 211.5 reduce-scatter.10
  1387.5 65.0 all-reduce.12
where the time goes:
time: 1620 us; the launch traced here: 1600 us
  waiting for transfers between devices  1120 us (69%)
  blocking collectives  312 us (19%)
  matrix products  80.5 us (5%)
  other arithmetic  33.1 us (2%)
  local copies, waits for them, and re-layouts  24.4 us (2%)
  between operations  18.3 us (1%)
    reduce_scatter x4, waiting for transfers between devices, forward(): local = lax.psum_scatter(dense, 'region', scatter_dimension=0, tiled=True)  848 us
    psum x4, waiting for transfers between devices, forward(): return lax.psum(local, 'slot').reshape(-1)  266 us
    psum x2, blocking collectives, body(): totals = lax.psum((square_sum, prior_sum), ('region', 'slot'))  157 us
    psum x2, blocking collectives, body(): sounding_total = lax.psum(sounding_part, 'region')  117 us
    dot_general x4, matrix products, forward(): jnp.einsum('sqkoc,sqkc->sqko', blocks, picked, precision=lax.Precision.HI...  61.5 us
  transfers between devices with their start and end apart: 9, of which 9 were waited for; matrix products, arithmetic and copies ran while one was open for 0% of the time, Pallas kernels for 0%

commit v1 on v0

v1 whole, which is shorter than its diff:
```python
import jax
import jax.numpy as jnp
from jax import lax
from jax.experimental import pallas as pl
from jax.experimental.pallas import tpu as pltpu
from jax.sharding import PartitionSpec as P

REGIONS = 32
SLOTS = 8
MOST = 8
BLOCK = 64
BLOCKS = REGIONS * MOST
CBLK = 512
LANES = 128
CHUNKS = 8
CHUNK_LANES = BLOCK * BLOCK // CHUNKS
MESH = pl.DeviceIdType.MESH
F32 = jnp.float32
BF16 = jnp.bfloat16

INDEX, FWD0, BACK0, FWD1, BACK1, FWD2, SUM0, SUM1, SUM2, GATHER0, GATHER1, LAST_SLOT, LAST_REGION = range(13)
EXCHANGES = 13


def iota(shape, axis):
    return lax.broadcasted_iota(jnp.int32, shape, axis)


def lane_region(lane):
    return (lane % LANES) // 4


def lane_place(lane):
    return (lane // LANES) * 4 + lane % 4


def pick(x, onehot, dims):
    high = x.astype(BF16)
    rest = x - high.astype(F32)
    middle = rest.astype(BF16)
    low = (rest - middle.astype(F32)).astype(BF16)
    pieces = jnp.concatenate([high, middle, low], axis=0)
    out = lax.dot_general(pieces, onehot, (dims, ((), ())), preferred_element_type=F32)
    return out[:BLOCK] + out[BLOCK : 2 * BLOCK] + out[2 * BLOCK :]


AS_IS = ((1,), (0,))
TURNED = ((1,), (1,))


def to_rows(x):
    return jnp.concatenate([x[:, :LANES], x[:, LANES:]], axis=0).T


def from_rows(x):
    y = x.T
    return jnp.concatenate([y[:BLOCK], y[BLOCK:]], axis=1)


def load_cells(ref):
    x = ref[...]
    a, b = x[:LANES].T, x[LANES:].T
    return jnp.concatenate([a[:BLOCK], b[:BLOCK], a[BLOCK:], b[BLOCK:]], axis=1)


def store_cells(x):
    a = jnp.concatenate([x[:, :LANES], x[:, 2 * LANES : 3 * LANES]], axis=0).T
    b = jnp.concatenate([x[:, LANES : 2 * LANES], x[:, 3 * LANES :]], axis=0).T
    return jnp.concatenate([a, b], axis=0)


def total(x):
    return jnp.sum(jnp.sum(x, axis=0, keepdims=True), axis=1, keepdims=True)


def kernel(
    flux, prior, precision, value, weight, foot, counts, obs_blocks, cell_blocks,
    increment, gradient,
    foot_in, foot_t, picked, part, cells, onehot_c, onehot_a, index_out, index_in,
    fwd_out, fwd_in, back_out, back_in, last_back_out, last_back_in,
    dense, sums, spread, last_spread, spread_out, last_spread_out,
    slot_out, slot_in, region_out, region_in,
    foot_sem, send_sem, recv_sem,
):
    me = lax.axis_index("region")
    slot = lax.axis_index("slot")

    def each(axis, count, mine, act):
        @pl.loop(1, count)
        def _(step):
            act({axis: lax.rem(mine + step, count)}, lax.rem(mine + step, count))

    barrier = pltpu.get_barrier_semaphore()

    def greet(device, _):
        pl.semaphore_signal(barrier, inc=1, device_id=device, device_id_type=MESH)

    each("region", REGIONS, me, greet)
    each("slot", SLOTS, slot, greet)

    def foot_copy(chunk):
        at = pl.ds(chunk * CHUNK_LANES, CHUNK_LANES)
        return pltpu.make_async_copy(foot.at[:, :, at], foot_in.at[:, :, at], foot_sem.at[chunk])

    for chunk in range(CHUNKS):
        foot_copy(chunk).start()

    def send(axis, exchange, source, target):
        count, mine = (REGIONS, me) if axis == "region" else (SLOTS, slot)

        def act(device, other):
            pltpu.make_async_remote_copy(
                src_ref=source(other),
                dst_ref=target.at[mine],
                send_sem=send_sem.at[exchange],
                recv_sem=recv_sem.at[exchange],
                device_id=device,
                device_id_type=MESH,
            ).start()

        each(axis, count, mine, act)

    def finish(axis, exchange, target):
        count, mine = (REGIONS, me) if axis == "region" else (SLOTS, slot)
        others = target.at[pl.ds(0, count - 1)]
        return pltpu.make_async_remote_copy(
            src_ref=others,
            dst_ref=others,
            send_sem=send_sem.at[exchange],
            recv_sem=recv_sem.at[exchange],
            device_id={axis: lax.rem(mine + 1, count)},
            device_id_type=MESH,
        )

    index = jnp.concatenate(
        [obs_blocks[...], jnp.zeros((REGIONS, LANES - MOST), jnp.int32)], axis=1
    )
    index_out[...] = index.reshape(REGIONS, 1, LANES)
    index_in[me] = index_out[me]
    pl.semaphore_wait(barrier, REGIONS + SLOTS - 2)
    send("region", INDEX, lambda p: index_out.at[p], index_in)

    lane = iota((REGIONS, BLOCKS), 1)
    of_region = lane_region(lane) == iota((REGIONS, BLOCKS), 0)
    by_place = (lane_place(iota((MOST, BLOCKS), 1)) == iota((MOST, BLOCKS), 0)).astype(F32)
    cell_index = jnp.dot(
        cell_blocks[...].astype(F32), by_place, precision=lax.Precision.HIGHEST,
        preferred_element_type=F32,
    )
    cell_index = jnp.sum(jnp.where(of_region, cell_index, 0.0), axis=0, keepdims=True)
    live = jnp.dot(
        counts[...].astype(F32), of_region.astype(F32), precision=lax.Precision.HIGHEST,
        preferred_element_type=F32,
    )
    live = lane_place(iota((1, BLOCKS), 1)).astype(F32) < live - 0.5
    cell_index = jnp.where(live, cell_index, -1.0)
    row = iota((CBLK, BLOCKS), 0)
    block = ((row % 256) * 2 + row // 256).astype(F32)
    onehot_c[...] = jnp.where(block == cell_index, 1.0, 0.0).astype(BF16)

    start = load_cells(flux)
    start_picked = pick(start, onehot_c[...], AS_IS)
    picked[...] = start_picked
    gap = start - load_cells(prior)
    prec = load_cells(precision)

    for chunk in range(CHUNKS):
        foot_copy(chunk).wait()

        @pl.loop(0, CHUNK_LANES // LANES)
        def _(step):
            column = chunk * (CHUNK_LANES // LANES) + step
            at = pl.ds(pl.multiple_of(column * LANES, LANES), LANES)
            for half in range(2):
                x = foot_in[:, half * 4 : half * 4 + 4, at].reshape(LANES, LANES).T
                foot_t[pl.ds(column * 2, 2), :, half * LANES : (half + 1) * LANES] = x.reshape(
                    2, BLOCK, LANES
                )

    finish("region", INDEX, index_in).wait_recv()
    arrived = index_in[...].reshape(REGIONS, LANES).astype(F32)
    row = iota((BLOCKS, REGIONS), 0)
    by_region = (lane_region(row) == iota((BLOCKS, REGIONS), 1)).astype(F32)
    target = jnp.dot(
        by_region, arrived, precision=lax.Precision.HIGHEST, preferred_element_type=F32
    )
    row = iota((BLOCKS, LANES), 0)
    target = jnp.where(lane_place(row) == iota((BLOCKS, LANES), 1), target, 0.0)
    target = jnp.sum(target, axis=1, keepdims=True)
    column = iota((BLOCKS, 256), 1)
    block = ((column % LANES) * 2 + column // LANES).astype(F32)
    onehot_a[...] = jnp.where(block == target, 1.0, 0.0).astype(BF16)

    def forward(step, fwd, reduce):
        @pl.loop(0, BLOCK // 8)
        def _(group):
            field = picked[...]
            rows = [
                jnp.sum(foot_t[group * 8 + i] * field, axis=0, keepdims=True) for i in range(8)
            ]
            part[pl.ds(pl.multiple_of(group * 8, 8), 8), :] = jnp.concatenate(rows, axis=0)

        fwd_out[step] = to_rows(part[...]).reshape(REGIONS, 4, LANES)
        fwd_in[step, me] = fwd_out[step, me]
        send("region", fwd, lambda p: fwd_out.at[step, p], fwd_in.at[step])
        finish("region", fwd, fwd_in.at[step]).wait_recv()
        came = from_rows(fwd_in[step].reshape(LANES, LANES))
        dense[step] = to_rows(pick(came, onehot_a[...], AS_IS)).reshape(SLOTS, 16, LANES)
        sums[step, slot] = dense[step, slot]
        send("slot", reduce, lambda s: dense.at[step, s], sums.at[step])
        finish("slot", reduce, sums.at[step]).wait_recv()
        return jnp.sum(sums[step], axis=0)

    def to_sources(rows):
        return to_rows(pick(from_rows(rows), onehot_a[...], TURNED)).reshape(REGIONS, 4, LANES)

    def adjoint(came):
        part[...] = from_rows(came)

        def step(group, acc):
            for i in range(8):
                o = group * 8 + i
                acc = acc + foot_t[o] * part[pl.ds(o, 1), :]
            return acc

        term = lax.fori_loop(0, BLOCK // 8, step, jnp.zeros((BLOCK, BLOCKS), F32))
        return pick(term, onehot_c[...], TURNED)

    mine = pl.ds(pl.multiple_of(slot * 16, 16), 16)
    left = iota((1, LANES), 1) < LANES // 2

    weighted = weight[mine, :] * (forward(0, FWD0, SUM0) - value[mine, :])
    spread_out[...] = weighted
    spread[slot] = weighted
    send("slot", GATHER0, lambda s: spread_out, spread)
    finish("slot", GATHER0, spread).wait_recv()
    back_out[...] = to_sources(spread[...].reshape(LANES, LANES))
    back_in[me] = back_out[me]
    send("region", BACK0, lambda p: back_out.at[p], back_in)
    finish("region", BACK0, back_in).wait_recv()
    first = adjoint(back_in[...].reshape(LANES, LANES)) + prec * gap
    cells[...] = first

    picked[...] = pick(first, onehot_c[...], AS_IS)
    numer, denom = total(first * first), total(prec * first * first)
    image = forward(1, FWD1, SUM1)
    weighted = weight[mine, :] * image
    scalars = jnp.where(left, numer, denom + total(weighted * image))
    last_spread_out[...] = jnp.concatenate(
        [weighted, scalars, jnp.zeros((7, LANES), F32)], axis=0
    )
    last_spread[slot] = last_spread_out[...]
    send("slot", GATHER1, lambda s: last_spread_out, last_spread)
    finish("slot", GATHER1, last_spread).wait_recv()
    last_back_out[:, :4, :] = to_sources(last_spread[:, :16, :].reshape(LANES, LANES))
    scalars = jnp.sum(last_spread[:, 16, :], axis=0, keepdims=True)
    last_back_out[:, 4:5, :] = jnp.broadcast_to(scalars.reshape(1, 1, LANES), (REGIONS, 1, LANES))
    last_back_in[me] = last_back_out[me]
    send("region", BACK1, lambda p: last_back_out.at[p], last_back_in)
    finish("region", BACK1, last_back_in).wait_recv()
    scalars = jnp.sum(last_back_in[:, 4, :], axis=0, keepdims=True)
    alpha = scalars[:, 0:1] / scalars[:, LANES // 2 : LANES // 2 + 1]
    first = cells[...]
    product = adjoint(last_back_in[:, :4, :].reshape(LANES, LANES)) + prec * first

    second = first - alpha * product
    picked[...] = pick(second, onehot_c[...], AS_IS)
    gradient[...] = store_cells(second)
    increment[...] = store_cells(alpha * first)
    numer, denom = total(second * second), total(prec * second * second)
    image = forward(2, FWD2, SUM2)
    denom = denom + total(weight[mine, :] * image * image)
    slot_out[...] = jnp.where(left, numer, denom)
    slot_in[slot] = slot_out[...]
    send("slot", LAST_SLOT, lambda s: slot_out, slot_in)
    finish("slot", LAST_SLOT, slot_in).wait_recv()
    region_out[...] = jnp.sum(slot_in[...], axis=0)
    region_in[me] = region_out[...]
    send("region", LAST_REGION, lambda p: region_out, region_in)
    finish("region", LAST_REGION, region_in).wait_recv()
    scalars = jnp.sum(region_in[...], axis=0)
    alpha = scalars[:, 0:1] / scalars[:, LANES // 2 : LANES // 2 + 1]
    increment[...] = -(increment[...] + alpha * gradient[...])

    for exchange, target in (
        (INDEX, index_in), (FWD0, fwd_in.at[0]), (BACK0, back_in), (FWD1, fwd_in.at[1]),
        (BACK1, last_back_in), (FWD2, fwd_in.at[2]), (LAST_REGION, region_in),
    ):
        finish("region", exchange, target).wait_send()
    for exchange, target in (
        (SUM0, sums.at[0]), (SUM1, sums.at[1]), (SUM2, sums.at[2]), (GATHER0, spread),
        (GATHER1, last_spread), (LAST_SLOT, slot_in),
    ):
        finish("slot", exchange, target).wait_send()


def body(
    flux, prior_flux, prior_precision, obs_value, obs_weight, footprint, counts, obs_blocks,
    cell_blocks,
):
    vmem = pl.BlockSpec(memory_space=pltpu.VMEM)
    cells = (256, LANES)
    increment, gradient = pl.pallas_call(
        kernel,
        out_shape=[jax.ShapeDtypeStruct(cells, F32)] * 2,
        in_specs=[vmem] * 5 + [pl.BlockSpec(memory_space=pl.ANY)] + [vmem] * 3,
        out_specs=[vmem] * 2,
        scratch_shapes=[
            pltpu.VMEM((REGIONS, MOST, BLOCK * BLOCK), F32),
            pltpu.VMEM((BLOCK, BLOCK, BLOCKS), F32),
            pltpu.VMEM((BLOCK, BLOCKS), F32),
            pltpu.VMEM((BLOCK, BLOCKS), F32),
            pltpu.VMEM((BLOCK, CBLK), F32),
            pltpu.VMEM((CBLK, BLOCKS), BF16),
            pltpu.VMEM((BLOCKS, 256), BF16),
            pltpu.VMEM((REGIONS, 1, LANES), jnp.int32),
            pltpu.VMEM((REGIONS, 1, LANES), jnp.int32),
            pltpu.VMEM((3, REGIONS, 4, LANES), F32),
            pltpu.VMEM((3, REGIONS, 4, LANES), F32),
            pltpu.VMEM((REGIONS, 4, LANES), F32),
            pltpu.VMEM((REGIONS, 4, LANES), F32),
            pltpu.VMEM((REGIONS, 5, LANES), F32),
            pltpu.VMEM((REGIONS, 5, LANES), F32),
            pltpu.VMEM((3, SLOTS, 16, LANES), F32),
            pltpu.VMEM((3, SLOTS, 16, LANES), F32),
            pltpu.VMEM((SLOTS, 16, LANES), F32),
            pltpu.VMEM((SLOTS, 24, LANES), F32),
            pltpu.VMEM((16, LANES), F32),
            pltpu.VMEM((24, LANES), F32),
            pltpu.VMEM((1, LANES), F32),
            pltpu.VMEM((SLOTS, 1, LANES), F32),
            pltpu.VMEM((1, LANES), F32),
            pltpu.VMEM((REGIONS, 1, LANES), F32),
            pltpu.SemaphoreType.DMA((CHUNKS,)),
            pltpu.SemaphoreType.DMA((EXCHANGES,)),
            pltpu.SemaphoreType.DMA((EXCHANGES,)),
        ],
        compiler_params=pltpu.CompilerParams(
            collective_id=0, has_side_effects=True, vmem_limit_bytes=40 * 1024 * 1024
        ),
        name="inversion",
    )(
        flux.reshape(cells),
        prior_flux.reshape(cells),
        prior_precision.reshape(cells),
        obs_value.reshape(LANES, LANES),
        obs_weight.reshape(LANES, LANES),
        footprint.reshape(REGIONS, MOST, BLOCK * BLOCK),
        counts.reshape(1, REGIONS),
        obs_blocks.reshape(REGIONS, MOST),
        cell_blocks.reshape(REGIONS, MOST),
    )
    return increment.reshape(flux.shape), gradient.reshape(flux.shape)


def solution(mesh):
    placed = (
        P("slot", "region"),
        P("slot", "region"),
        P("slot", "region"),
        P("region"),
        P("region"),
        P("slot", "region", None, None, None),
        P("slot", "region", None),
        P("slot", "region", None, None),
        P("slot", "region", None, None),
    )
    return jax.shard_map(
        body,
        mesh=mesh,
        in_specs=placed,
        out_specs=(P("slot", "region"), P("slot", "region")),
        check_vma=False,
    )
```

time: 1620 us -> 90.6 us (0.06); the launches traced: 1600 us -> 90.3 us
  waiting for transfers between devices: 1120 us -> 0 us
  blocking collectives: 312 us -> 0 us
  matrix products: 80.5 us -> 0 us
  Pallas kernels: 0 us -> 79.5 us
  other arithmetic: 33.1 us -> 0 us
  between operations: 18.3 us -> 0.65 us
    reduce_scatter x4 -> x0, waiting for transfers between devices: 848 us -> none  [forward(): local = lax.psum_scatter(dense, 'region', scatter_dimension=0, tiled=True)]
    psum x4 -> x0, blocking collectives: 274 us -> none  [the longest x2 157 us: body(): totals = lax.psum((square_sum, prior_sum), ('region', 'slot'))]
    psum x4 -> x0, waiting for transfers between devices: 266 us -> none  [forward(): return lax.psum(local, 'slot').reshape(-1)]
    dot_general x6 -> x0, matrix products: 80.5 us -> none  [the longest x4 61.5 us: forward(): jnp.einsum('sqkoc,sqkc->sqko', blocks, picked, precision=lax.Precision.HI...]
    pallas_call x0 -> x1, Pallas kernels: none -> 79.5 us  [body(): pl.pallas_call(kernel, out_shape=[jax.ShapeDtypeStruct(cells, F32)] * 2,...]
    all_to_all x2 -> x0, blocking collectives: 38.4 us -> none  [the longest x1 20.2 us: body(): lax.all_to_all(obs_blocks, 'region', split_axis=2, concat_axis=1, tiled=T...]
    scatter-add x6 -> x0, other arithmetic: 18.2 us -> none  [the longest x4 14.8 us: forward(): jax.ops.segment_sum(part.reshape(-1, BLOCK), dense_rows, regions * obs_co...]
  transfers between devices with their start and end apart: 9 -> 0, of which waited for: 9 -> 0; matrix products, arithmetic and copies ran while one was open for 0% -> 0% of each run, Pallas kernels for 0% -> 0%
where the time goes in v1:
time: 90.6 us; the launch traced here: 90.3 us
  Pallas kernels  79.5 us (88%)
  local copies, waits for them, and re-layouts  10.1 us (11%)
    pallas_call x1, Pallas kernels, body(): pl.pallas_call(kernel, out_shape=[jax.ShapeDtypeStruct(cells, F32)] * 2,...  79.5 us
    unnamed x18, local copies, waits for them, and re-layouts  10.1 us

profile of v1, /device:TPU:1, one launch (start us, length us, event | category | flops | bytes accessed | tf_op | source)
XLA Modules:
  0.0 90.3 jit_solution(3566212024841396065)
XLA Ops:
  0.6 0.8 copy.11
  1.4 0.8 copy.12
  2.2 0.0 copy-start
  2.2 2.2 %copy-done = f32[1,1,32,8,4096]{4,3,2,1,0:T(8,128)S(1)} copy-done((f32[1,1,32,8,4096]{4,3,2,1,0:T(8,128)S(1)}, f32[1,1,32,8,4096]{4,3,2,1,0:T(8,128)}, u32[]{:S(2)}) %copy-start) | copy-done | bytes 4194328
  4.3 0.0 copy-start.1
  4.3 0.9 copy-done.1
  5.2 0.0 copy-start.2
  5.2 0.9 copy-done.2
  6.2 0.0 copy-start.3
  6.2 0.9 copy-done.3
  7.1 0.0 copy-start.4
  7.1 0.8 copy-done.4
  7.9 0.0 copy-start.5
  7.9 0.8 copy-done.5
  8.7 0.0 copy-start.6
  8.7 0.7 copy-done.6
  9.4 79.5 %inversion.1 = (f32[256,128]{1,0:T(8,128)S(1)}, f32[256,128]{1,0:T(8,128)S(1)}) custom-call(f32[256,128]{1,0:T(8,128)S(1)} %bitcast.12, f32[256,128]{1,0:T(8,128)S(1)} %bitcast.13, f32[256,128]{1,0:T(8,128)S(1)} %bitcast.14, f32[128,128]{1,0:T(8,128)S(1)} %bitcast.17, f32[128,128]{1,0:T(8,128)S(1)} %bitcast.18, f32[32,8,4096]{2,1,0:T(8,128)S(1)} %bitcast.11, ...), custom_call_target="tpu_custom_call" | custom-call | tf_op jit(solution)/shard_map/inversion/pallas_call | solution.py:303
  88.9 0.7 copy.15
  89.6 0.7 copy.16
Async XLA Ops:
  2.2 2.2 %copy-start = (f32[1,1,32,8,4096]{4,3,2,1,0:T(8,128)S(1)}, f32[1,1,32,8,4096]{4,3,2,1,0:T(8,128)}, u32[]{:S(2)}) copy-start(f32[1,1,32,8,4096]{4,3,2,1,0:T(8,128)} %param.14) | copy-start | bytes 12582916
  4.3 0.9 %copy-start.1 = (f32[1,32768]{1,0:T(1,128)S(1)}, f32[1,32768]{1,0:T(1,128)}, u32[]{:S(2)}) copy-start(f32[1,32768]{1,0:T(1,128)} %param.9) | copy-start | bytes 393220
  5.2 0.9 %copy-start.2 = (f32[1,32768]{1,0:T(1,128)S(1)}, f32[1,32768]{1,0:T(1,128)}, u32[]{:S(2)}) copy-start(f32[1,32768]{1,0:T(1,128)} %param.10) | copy-start | bytes 393220
  6.2 0.9 %copy-start.3 = (f32[1,32768]{1,0:T(1,128)S(1)}, f32[1,32768]{1,0:T(1,128)}, u32[]{:S(2)}) copy-start(f32[1,32768]{1,0:T(1,128)} %param.11) | copy-start | bytes 393220
  7.1 0.8 copy-start.4
  7.9 0.8 copy-start.5
  8.7 0.7 copy-start.6

commit v2 on v0

v2 whole, which is shorter than its diff:
```python
import jax
import jax.numpy as jnp
from jax import lax
from jax.experimental import pallas as pl
from jax.experimental.pallas import tpu as pltpu
from jax.sharding import PartitionSpec as P

REGIONS = 32
SLOTS = 8
MOST = 8
BLOCK = 64
BLOCKS = REGIONS * MOST
CBLK = 512
OBLK = 256
LANES = 128
CHIPS = 128
SHARE = 16
PAIRS = SHARE // 2
TILES = BLOCK // 2
MESH = pl.DeviceIdType.MESH
F32 = jnp.float32
BF16 = jnp.bfloat16
AS_IS = ((1,), (0,))
TURNED = ((1,), (1,))

FWD, BACK, LAST, CORE = (0, 1, 2), (3, 4), 5, (6, 7, 8)
EXCHANGES = 9


def hops(step):
    z, x, y = step
    return min(z, 8 - z) + min(x, 4 - x) + min(y, 4 - y)


STEPS = sorted(
    [(z, x, y) for z in range(8) for x in range(4) for y in range(4) if z or x or y],
    key=lambda step: (-hops(step), step),
)


def iota(shape, axis):
    return lax.broadcasted_iota(jnp.int32, shape, axis)


def pick(x, onehot, dims):
    high = x.astype(BF16)
    rest = x - high.astype(F32)
    middle = rest.astype(BF16)
    low = (rest - middle.astype(F32)).astype(BF16)
    pieces = jnp.concatenate([high, middle, low], axis=0)
    out = lax.dot_general(pieces, onehot, (dims, ((), ())), preferred_element_type=F32)
    rows = x.shape[0]
    return out[:rows] + out[rows : 2 * rows] + out[2 * rows :]


def load_cells(ref):
    x = ref[...]
    a, b = x[:LANES].T, x[LANES:].T
    return jnp.concatenate([a[:BLOCK], b[:BLOCK], a[BLOCK:], b[BLOCK:]], axis=1)


def store_cells(x):
    a = jnp.concatenate([x[:, :LANES], x[:, 2 * LANES : 3 * LANES]], axis=0).T
    b = jnp.concatenate([x[:, LANES : 2 * LANES], x[:, 3 * LANES :]], axis=0).T
    return jnp.concatenate([a, b], axis=0)


def total(x):
    return jnp.sum(jnp.sum(x, axis=0, keepdims=True), axis=1, keepdims=True)


def side_by_side(x):
    return jnp.concatenate([x[SHARE * k : SHARE * (k + 1)] for k in range(MOST)], axis=1)


def stacked(x):
    return jnp.concatenate([x[:, LANES * k : LANES * (k + 1)] for k in range(MOST)], axis=0)


def kernel(
    flux_hbm, prior_hbm, precision_hbm, value_hbm, weight_hbm, foot, counts_hbm, obs_hbm, cell_hbm,
    first_out, product_out, alphas,
    flux, prior, precision, value, weight, counts, obs_blocks, cell_blocks,
    foot_in, foot_t, picked, part, cells, prec, gap, onehot_c, onehot_a, observed,
    first_fwd_out, first_fwd_in, fwd_out, fwd_in, back_out, back_in, last_back_out, last_back_in,
    core_out, core_in, last_out, last_in,
    foot_sem, in_sem, send_sem, recv_sem,
):
    region, slot = lax.axis_index("region"), lax.axis_index("slot")
    y, core = lax.div(slot, 2), lax.rem(slot, 2)
    z, x = lax.div(region, 4), lax.rem(region, 4)
    me = y * REGIONS + region
    partner = {"slot": slot + 1 - 2 * core}
    at_z = [lax.rem(z + step, 8) * 4 for step in range(8)]
    at_x = [lax.rem(x + step, 4) for step in range(4)]
    at_y = [lax.rem(y + step, 4) for step in range(4)]
    slot_at = [at * 2 + core for at in at_y]
    row_at = [at * REGIONS for at in at_y]

    loads = [
        pltpu.make_async_copy(source, target, in_sem.at[i])
        for i, (source, target) in enumerate((
            (obs_hbm, obs_blocks), (cell_hbm, cell_blocks), (counts_hbm, counts), (flux_hbm, flux),
            (prior_hbm, prior), (precision_hbm, precision), (value_hbm, value), (weight_hbm, weight),
        ))
    ]

    def foot_copy(tile):
        return pltpu.make_async_copy(
            foot.at[:, pl.ds(tile * LANES, LANES)],
            foot_in.at[pl.ds(tile * BLOCKS, BLOCKS), :],
            foot_sem.at[tile],
        )

    starts = loads[:4] + [
        foot_copy(share * PAIRS + pair) for pair in range(PAIRS) for share in range(4)
    ] + loads[4:]
    barrier = pltpu.get_barrier_semaphore()
    for i, (dz, dx, dy) in enumerate(STEPS):
        pl.semaphore_signal(
            barrier, inc=1, device_id={"region": at_z[dz] + at_x[dx], "slot": slot_at[dy]},
            device_id_type=MESH,
        )
        if i % 2 == 1 and starts:
            starts.pop(0).start()
    pl.semaphore_signal(barrier, inc=1, device_id=partner, device_id_type=MESH)

    def remote(source, target, exchange, device):
        return pltpu.make_async_remote_copy(
            src_ref=source,
            dst_ref=target,
            send_sem=send_sem.at[exchange],
            recv_sem=recv_sem.at[exchange],
            device_id=device,
            device_id_type=MESH,
        )

    def send(exchange, source, target):
        for dz, dx, dy in STEPS:
            there = at_z[dz] + at_x[dx]
            remote(
                source(row_at[dy] + there), target.at[me], exchange,
                {"region": there, "slot": slot_at[dy]},
            ).start()

    def finish(exchange, target):
        others = target.at[pl.ds(0, CHIPS - 1)]
        return remote(others, others, exchange, partner)

    lane = iota((REGIONS, BLOCKS), 1)
    of_region = lane % REGIONS == iota((REGIONS, BLOCKS), 0)
    of_place = iota((MOST, BLOCKS), 1) // REGIONS == iota((MOST, BLOCKS), 0)
    loads[1].wait()
    loads[2].wait()
    cell_index = jnp.dot(
        cell_blocks[...].astype(F32), of_region.astype(F32), precision=lax.Precision.HIGHEST,
        preferred_element_type=F32,
    )
    cell_index = jnp.sum(jnp.where(of_place, cell_index, 0.0), axis=0, keepdims=True)
    live = jnp.dot(
        counts[...].astype(F32), of_region.astype(F32), precision=lax.Precision.HIGHEST,
        preferred_element_type=F32,
    )
    live = (iota((1, BLOCKS), 1) // REGIONS).astype(F32) < live - 0.5
    cell_index = jnp.where(live, cell_index, -1.0)
    row = iota((CBLK, BLOCKS), 0)
    block = ((row % 256) * 2 + row // 256).astype(F32)
    onehot_c[...] = jnp.where(block == cell_index, 1.0, 0.0).astype(BF16)

    group = iota((1, LANES), 1) // REGIONS

    def pick_cells(field):
        found = pick(field, onehot_c[...], AS_IS)
        for k in range(MOST):
            half = found[:, k // 4 * LANES : (k // 4 + 1) * LANES]
            half = jnp.where(group == k % 4, half, 0.0)
            half = half + pltpu.roll(half, 2 * REGIONS, 1)
            picked[k] = half + pltpu.roll(half, REGIONS, 1)

    loads[3].wait()
    pick_cells(load_cells(flux))

    loads[0].wait()
    index = jnp.concatenate(
        [obs_blocks[...].astype(F32), jnp.zeros((MOST, LANES - REGIONS), F32)], axis=1
    )
    index = jnp.concatenate([index, jnp.zeros((LANES - MOST, LANES), F32)], axis=0).T
    index = jnp.concatenate([index[:REGIONS]] * 4, axis=0)
    first_fwd_out[:, 1:, :] = index.reshape(CHIPS, 1, LANES)

    for pair in range(PAIRS):
        for share in range(4):
            foot_copy(share * PAIRS + pair).wait()

        @pl.loop(0, MOST)
        def _(k):
            block = [
                foot_in[pl.ds((share * PAIRS + pair) * BLOCKS + k, REGIONS, stride=MOST), :]
                for share in range(4)
            ]
            block = jnp.concatenate(block, axis=0).T
            foot_t[pl.ds(k * SHARE + 2 * pair, 2)] = block.reshape(2, BLOCK, LANES)

    def partials():
        @pl.loop(0, MOST)
        def _(k):
            field = picked[k]
            rows = [
                jnp.sum(foot_t[k * SHARE + i] * field, axis=0, keepdims=True) for i in range(SHARE)
            ]
            part[pl.ds(pl.multiple_of(k * SHARE, SHARE), SHARE), :] = jnp.concatenate(rows, axis=0)

        return part[...].T.reshape(CHIPS, 1, LANES)

    def summed(came, step, numer, denom):
        dense = pick(side_by_side(came.T), onehot_a[...], AS_IS)
        scalars = jnp.where(iota((8, OBLK), 1) < LANES, numer, denom)
        core_out[step] = jnp.concatenate([dense, scalars], axis=0)
        copy = remote(core_out.at[step], core_in.at[step], CORE[step], partner)
        copy.start()
        copy.wait_recv()
        both = core_out[step] + core_in[step]
        scalars = both[SHARE : SHARE + 1]
        return both[:SHARE], scalars[:, :1], scalars[:, LANES : LANES + 1]

    def to_sources(weighted):
        return stacked(pick(weighted, onehot_a[...], TURNED)).T.reshape(CHIPS, 1, LANES)

    def adjoint(came):
        part[...] = came.T
        halves = []
        for half in range(2):
            merged = jnp.zeros((BLOCK, LANES), F32)
            for place in range(4):
                k = half * 4 + place
                acc = foot_t[k * SHARE] * part[k * SHARE : k * SHARE + 1, :]
                for i in range(1, SHARE):
                    at = k * SHARE + i
                    acc = acc + foot_t[at] * part[at : at + 1, :]
                acc = acc + pltpu.roll(acc, 2 * REGIONS, 1)
                acc = acc + pltpu.roll(acc, REGIONS, 1)
                merged = jnp.where(group == place, acc, merged)
            halves.append(merged)
        return pick(jnp.concatenate(halves, axis=1), onehot_c[...], TURNED)

    left = iota((1, LANES), 1) < LANES // 2

    def ratio(rows):
        scalars = jnp.sum(rows, axis=0, keepdims=True)
        return scalars[:, :1] / scalars[:, LANES // 2 : LANES // 2 + 1]

    first_fwd_out[:, :1, :] = partials()
    first_fwd_in[me] = first_fwd_out[me]
    pl.semaphore_wait(barrier, CHIPS)
    send(FWD[0], lambda chip: first_fwd_out.at[chip], first_fwd_in)
    for load in loads[4:]:
        load.wait()
    gap[...] = load_cells(flux) - load_cells(prior)
    prec[...] = load_cells(precision)
    observed[0] = value[...].T.reshape(2, BLOCK, LANES)
    observed[1] = weight[...].T.reshape(2, BLOCK, LANES)
    mine = pl.ds(pl.multiple_of(y * SHARE, SHARE), SHARE)
    seen = jnp.concatenate([observed[0, 0, mine, :], observed[0, 1, mine, :]], axis=1)
    weights = jnp.concatenate([observed[1, 0, mine, :], observed[1, 1, mine, :]], axis=1)
    finish(FWD[0], first_fwd_in).wait_recv()
    index = first_fwd_in[:, 1, :]
    column = iota((LANES, OBLK), 1)
    block = ((column % LANES) * 2 + column // LANES).astype(F32)
    for k in range(MOST):
        onehot_a[k * LANES : (k + 1) * LANES, :] = jnp.where(
            index[:, k : k + 1] == block, 1.0, 0.0
        ).astype(BF16)
    image, _, _ = summed(first_fwd_in[:, 0, :], 0, 0.0, 0.0)
    back_out[...] = to_sources(weights * (image - seen))
    back_in[me] = back_out[me]
    send(BACK[0], lambda chip: back_out.at[chip], back_in)
    finish(BACK[0], back_in).wait_recv()
    first = adjoint(back_in[...].reshape(CHIPS, LANES)) + prec[...] * gap[...]
    cells[...] = first

    pick_cells(first)
    fwd_out[0] = partials()
    fwd_in[0, me] = fwd_out[0, me]
    send(FWD[1], lambda chip: fwd_out.at[0, chip], fwd_in.at[0])
    first = cells[...]
    first_out[...] = store_cells(first)
    square = first * first
    numer, denom = total(square), total(prec[...] * square)
    finish(FWD[1], fwd_in.at[0]).wait_recv()
    image, numer, denom = summed(fwd_in[0].reshape(CHIPS, LANES), 1, numer, denom)
    weighted = weights * image
    last_back_out[:, :1, :] = to_sources(weighted)
    scalars = jnp.where(left, numer, denom + total(weighted * image))
    last_back_out[:, 1:, :] = jnp.broadcast_to(scalars.reshape(1, 1, LANES), (CHIPS, 1, LANES))
    last_back_in[me] = last_back_out[me]
    send(BACK[1], lambda chip: last_back_out.at[chip], last_back_in)
    finish(BACK[1], last_back_in).wait_recv()
    first = cells[...]
    product = adjoint(last_back_in[:, 0, :]) + prec[...] * first
    alpha = ratio(last_back_in[:, 1, :])

    second = first - alpha * product
    cells[...] = second
    pick_cells(second)
    fwd_out[1] = partials()
    fwd_in[1, me] = fwd_out[1, me]
    send(FWD[2], lambda chip: fwd_out.at[1, chip], fwd_in.at[1])
    product_out[...] = store_cells(product)
    second = cells[...]
    square = second * second
    numer, denom = total(square), total(prec[...] * square)
    finish(FWD[2], fwd_in.at[1]).wait_recv()
    image, numer, denom = summed(fwd_in[1].reshape(CHIPS, LANES), 2, numer, denom)
    last_out[...] = jnp.where(left, numer, denom + total(weights * image * image))
    last_in[me] = last_out[...]
    send(LAST, lambda chip: last_out, last_in)
    finish(LAST, last_in).wait_recv()
    alphas[...] = jnp.where(left, alpha, ratio(last_in[...].reshape(CHIPS, LANES)))

    for exchange, target in (
        (FWD[0], first_fwd_in), (BACK[0], back_in), (FWD[1], fwd_in.at[0]),
        (BACK[1], last_back_in), (FWD[2], fwd_in.at[1]), (LAST, last_in),
    ):
        finish(exchange, target).wait_send()
    for step in range(3):
        remote(core_out.at[step], core_in.at[step], CORE[step], partner).wait_send()


def body(
    flux, prior_flux, prior_precision, obs_value, obs_weight, footprint, counts, obs_blocks,
    cell_blocks,
):
    cells = (256, LANES)
    message, double = (CHIPS, 1, LANES), (CHIPS, 2, LANES)
    first, product, alphas = pl.pallas_call(
        kernel,
        out_shape=[
            jax.ShapeDtypeStruct(cells, F32),
            jax.ShapeDtypeStruct(cells, F32),
            jax.ShapeDtypeStruct((1, LANES), F32),
        ],
        in_specs=[pl.BlockSpec(memory_space=pltpu.HBM)] * 9,
        out_specs=[pl.BlockSpec(memory_space=pltpu.VMEM)] * 3,
        scratch_shapes=[
            pltpu.VMEM(cells, F32),
            pltpu.VMEM(cells, F32),
            pltpu.VMEM(cells, F32),
            pltpu.VMEM((LANES, LANES), F32),
            pltpu.VMEM((LANES, LANES), F32),
            pltpu.VMEM((1, REGIONS), jnp.int32),
            pltpu.VMEM((MOST, REGIONS), jnp.int32),
            pltpu.VMEM((MOST, REGIONS), jnp.int32),
            pltpu.VMEM((TILES * BLOCKS, LANES), F32),
            pltpu.VMEM((MOST * SHARE, BLOCK, LANES), F32),
            pltpu.VMEM((MOST, BLOCK, LANES), F32),
            pltpu.VMEM((LANES, LANES), F32),
            pltpu.VMEM((BLOCK, CBLK), F32),
            pltpu.VMEM((BLOCK, CBLK), F32),
            pltpu.VMEM((BLOCK, CBLK), F32),
            pltpu.VMEM((CBLK, BLOCKS), BF16),
            pltpu.VMEM((MOST * LANES, OBLK), BF16),
            pltpu.VMEM((2, 2, BLOCK, LANES), F32),
            pltpu.VMEM(double, F32),
            pltpu.VMEM(double, F32),
            pltpu.VMEM((2, *message), F32),
            pltpu.VMEM((2, *message), F32),
            pltpu.VMEM(message, F32),
            pltpu.VMEM(message, F32),
            pltpu.VMEM(double, F32),
            pltpu.VMEM(double, F32),
            pltpu.VMEM((3, SHARE + 8, OBLK), F32),
            pltpu.VMEM((3, SHARE + 8, OBLK), F32),
            pltpu.VMEM((1, LANES), F32),
            pltpu.VMEM(message, F32),
            pltpu.SemaphoreType.DMA((TILES,)),
            pltpu.SemaphoreType.DMA((8,)),
            pltpu.SemaphoreType.DMA((EXCHANGES,)),
            pltpu.SemaphoreType.DMA((EXCHANGES,)),
        ],
        compiler_params=pltpu.CompilerParams(
            collective_id=0, has_side_effects=True, vmem_limit_bytes=60 * 1024 * 1024
        ),
        name="inversion",
    )(
        flux.reshape(cells),
        prior_flux.reshape(cells),
        prior_precision.reshape(cells),
        obs_value.reshape(LANES, LANES),
        obs_weight.reshape(LANES, LANES),
        footprint.reshape(BLOCKS, BLOCK * BLOCK),
        counts.reshape(1, REGIONS),
        obs_blocks.reshape(REGIONS, MOST).T,
        cell_blocks.reshape(REGIONS, MOST).T,
    )
    alpha, last_alpha = alphas[0, 0], alphas[0, LANES - 1]
    gradient = first - alpha * product
    increment = -(alpha * first + last_alpha * gradient)
    return increment.reshape(flux.shape), gradient.reshape(flux.shape)


def solution(mesh):
    placed = (
        P("slot", "region"),
        P("slot", "region"),
        P("slot", "region"),
        P("region"),
        P("region"),
        P("slot", "region", None, None, None),
        P("slot", "region", None),
        P("slot", "region", None, None),
        P("slot", "region", None, None),
    )
    return jax.shard_map(
        body,
        mesh=mesh,
        in_specs=placed,
        out_specs=(P("slot", "region"), P("slot", "region")),
        check_vma=False,
    )
```

time: 1620 us -> 71.7 us (0.04); the launches traced: 1600 us -> 71.6 us
  waiting for transfers between devices: 1120 us -> 0 us
  blocking collectives: 312 us -> 0 us
  matrix products: 80.5 us -> 0 us
  Pallas kernels: 0 us -> 66.7 us
  other arithmetic: 33.1 us -> 2.94 us
  local copies, waits for them, and re-layouts: 24.4 us -> 1.34 us
  between operations: 18.3 us -> 0.64 us
    reduce_scatter x4 -> x0, waiting for transfers between devices: 848 us -> none  [forward(): local = lax.psum_scatter(dense, 'region', scatter_dimension=0, tiled=True)]
    psum x4 -> x0, blocking collectives: 274 us -> none  [the longest x2 157 us: body(): totals = lax.psum((square_sum, prior_sum), ('region', 'slot'))]
    psum x4 -> x0, waiting for transfers between devices: 266 us -> none  [forward(): return lax.psum(local, 'slot').reshape(-1)]
    dot_general x6 -> x0, matrix products: 80.5 us -> none  [the longest x4 61.5 us: forward(): jnp.einsum('sqkoc,sqkc->sqko', blocks, picked, precision=lax.Precision.HI...]
    pallas_call x0 -> x1, Pallas kernels: none -> 66.7 us  [body(): pl.pallas_call(kernel, out_shape=[jax.ShapeDtypeStruct(cells, F32), jax.S...]
    all_to_all x2 -> x0, blocking collectives: 38.4 us -> none  [the longest x1 20.2 us: body(): lax.all_to_all(obs_blocks, 'region', split_axis=2, concat_axis=1, tiled=T...]
    scatter-add x6 -> x0, other arithmetic: 18.2 us -> none  [the longest x4 14.8 us: forward(): jax.ops.segment_sum(part.reshape(-1, BLOCK), dense_rows, regions * obs_co...]
  transfers between devices with their start and end apart: 9 -> 0, of which waited for: 9 -> 0; matrix products, arithmetic and copies ran while one was open for 0% -> 0% of each run, Pallas kernels for 0% -> 0%
where the time goes in v2:
time: 71.7 us; the launch traced here: 71.6 us
  Pallas kernels  66.7 us (93%)
  other arithmetic  2.94 us (4%)
  local copies, waits for them, and re-layouts  1.34 us (2%)
    pallas_call x1, Pallas kernels, body(): pl.pallas_call(kernel, out_shape=[jax.ShapeDtypeStruct(cells, F32), jax.S...  66.7 us
    sub x1, other arithmetic, body(): gradient = first - alpha * product  2.94 us

profile of v2, /device:TPU:1, one launch (start us, length us, event | category | flops | bytes accessed | tf_op | source)
XLA Modules:
  0.0 71.6 jit_solution(13241377215623032143)
XLA Ops:
  0.6 66.7 %inversion.1 = (f32[256,128]{1,0:T(8,128)}, f32[256,128]{1,0:T(8,128)}, f32[1,128]{1,0:T(1,128)}) custom-call(f32[256,128]{1,0:T(8,128)} %bitcast.18, f32[256,128]{1,0:T(8,128)} %bitcast.19, f32[256,128]{1,0:T(8,128)} %bitcast.20, f32[128,128]{1,0:T(8,128)} %bitcast.23, f32[128,128]{1,0:T(8,128)} %bitcast.24, f32[256,4096]{1,0:T(8,128)} %bitcast.17, ...), custom_call_target="tpu_custom_call" | custom-call | tf_op jit(solution)/shard_map/inversion/pallas_call | solution.py:335
  67.3 1.3 %fusion = (f32[1,1]{1,0:T(1,128)}, f32[1,1]{1,0:T(1,128)}) fusion(f32[1,128]{1,0:T(1,128)} %get-tuple-element.5), kind=kLoop, calls=%fused_computation.2 | loop fusion | bytes 16 | tf_op jit(solution)/shard_map/slice | solution.py:395
  68.7 2.9 %multiply_subtract_fusion = (f32[256,128]{1,0:T(8,128)}, f32[256,128]{1,0:T(8,128)}) fusion(f32[256,128]{1,0:T(8,128)} %get-tuple-element.6, f32[256,128]{1,0:T(8,128)} %get-tuple-element.7, f32[]{:T(128)} %bitcast.11, f32[]{:T(128)} %bitcast.12), kind=kLoop, calls=%fused_computation.1 | loop fusion | flops 196608 | bytes 524296 | tf_op jit(solution)/shard_map/sub | solution.py:396

commit v3 on v2

--- a/solution.py
+++ b/solution.py
@@ -79,12 +79,12 @@
 
 def kernel(
     flux_hbm, prior_hbm, precision_hbm, value_hbm, weight_hbm, foot, counts_hbm, obs_hbm, cell_hbm,
-    first_out, product_out, alphas,
+    increment, gradient_hbm,
     flux, prior, precision, value, weight, counts, obs_blocks, cell_blocks,
     foot_in, foot_t, picked, part, cells, prec, gap, onehot_c, onehot_a, observed,
     first_fwd_out, first_fwd_in, fwd_out, fwd_in, back_out, back_in, last_back_out, last_back_in,
-    core_out, core_in, last_out, last_in,
-    foot_sem, in_sem, send_sem, recv_sem,
+    core_out, core_in, last_out, last_in, gradient,
+    foot_sem, in_sem, send_sem, recv_sem, out_sem,
 ):
     region, slot = lax.axis_index("region"), lax.axis_index("slot")
     y, core = lax.div(slot, 2), lax.rem(slot, 2)
@@ -192,7 +192,7 @@
         for share in range(4):
             foot_copy(share * PAIRS + pair).wait()
 
-        @pl.loop(0, MOST)
+        @pl.loop(0, MOST, unroll=MOST)
         def _(k):
             block = [
                 foot_in[pl.ds((share * PAIRS + pair) * BLOCKS + k, REGIONS, stride=MOST), :]
@@ -283,7 +283,7 @@
     fwd_in[0, me] = fwd_out[0, me]
     send(FWD[1], lambda chip: fwd_out.at[0, chip], fwd_in.at[0])
     first = cells[...]
-    first_out[...] = store_cells(first)
+    increment[...] = store_cells(first)
     square = first * first
     numer, denom = total(square), total(prec[...] * square)
     finish(FWD[1], fwd_in.at[0]).wait_recv()
@@ -305,8 +305,11 @@
     fwd_out[1] = partials()
     fwd_in[1, me] = fwd_out[1, me]
     send(FWD[2], lambda chip: fwd_out.at[1, chip], fwd_in.at[1])
-    product_out[...] = store_cells(product)
     second = cells[...]
+    gradient[...] = store_cells(second)
+    result = pltpu.make_async_copy(gradient, gradient_hbm, out_sem)
+    result.start()
+    increment[...] = increment[...] * alpha
     square = second * second
     numer, denom = total(square), total(prec[...] * square)
     finish(FWD[2], fwd_in.at[1]).wait_recv()
@@ -315,7 +318,9 @@
     last_in[me] = last_out[...]
     send(LAST, lambda chip: last_out, last_in)
     finish(LAST, last_in).wait_recv()
-    alphas[...] = jnp.where(left, alpha, ratio(last_in[...].reshape(CHIPS, LANES)))
+    alpha = ratio(last_in[...].reshape(CHIPS, LANES))
+    increment[...] = -(increment[...] + alpha * gradient[...])
+    result.wait()
 
     for exchange, target in (
         (FWD[0], first_fwd_in), (BACK[0], back_in), (FWD[1], fwd_in.at[0]),
@@ -326,21 +331,28 @@
         remote(core_out.at[step], core_in.at[step], CORE[step], partner).wait_send()
 
 
+def hand_over(a, b, a_out, b_out, a_held, b_held, sem):
+    both = ((a, a_held, a_out, 0), (b, b_held, b_out, 1))
+    for source, held, _, i in both:
+        pltpu.make_async_copy(source, held, sem.at[i]).start()
+    for source, held, target, i in both:
+        pltpu.make_async_copy(source, held, sem.at[i]).wait()
+        pltpu.make_async_copy(held, target, sem.at[i + 2]).start()
+    for _, held, target, i in both:
+        pltpu.make_async_copy(held, target, sem.at[i + 2]).wait()
+
+
 def body(
     flux, prior_flux, prior_precision, obs_value, obs_weight, footprint, counts, obs_blocks,
     cell_blocks,
 ):
     cells = (256, LANES)
     message, double = (CHIPS, 1, LANES), (CHIPS, 2, LANES)
-    first, product, alphas = pl.pallas_call(
+    results = pl.pallas_call(
         kernel,
-        out_shape=[
-            jax.ShapeDtypeStruct(cells, F32),
-            jax.ShapeDtypeStruct(cells, F32),
-            jax.ShapeDtypeStruct((1, LANES), F32),
-        ],
+        out_shape=[jax.ShapeDtypeStruct(cells, F32)] * 2,
         in_specs=[pl.BlockSpec(memory_space=pltpu.HBM)] * 9,
-        out_specs=[pl.BlockSpec(memory_space=pltpu.VMEM)] * 3,
+        out_specs=[pl.BlockSpec(memory_space=pltpu.VMEM), pl.BlockSpec(memory_space=pltpu.HBM)],
         scratch_shapes=[
             pltpu.VMEM(cells, F32),
             pltpu.VMEM(cells, F32),
@@ -372,10 +384,12 @@
             pltpu.VMEM((3, SHARE + 8, OBLK), F32),
             pltpu.VMEM((1, LANES), F32),
             pltpu.VMEM(message, F32),
+            pltpu.VMEM(cells, F32),
             pltpu.SemaphoreType.DMA((TILES,)),
             pltpu.SemaphoreType.DMA((8,)),
             pltpu.SemaphoreType.DMA((EXCHANGES,)),
             pltpu.SemaphoreType.DMA((EXCHANGES,)),
+            pltpu.SemaphoreType.DMA,
         ],
         compiler_params=pltpu.CompilerParams(
             collective_id=0, has_side_effects=True, vmem_limit_bytes=60 * 1024 * 1024
@@ -392,9 +406,15 @@
         obs_blocks.reshape(REGIONS, MOST).T,
         cell_blocks.reshape(REGIONS, MOST).T,
     )
-    alpha, last_alpha = alphas[0, 0], alphas[0, LANES - 1]
-    gradient = first - alpha * product
-    increment = -(alpha * first + last_alpha * gradient)
+    hbm = [pl.BlockSpec(memory_space=pltpu.HBM)] * 2
+    increment, gradient = pl.pallas_call(
+        hand_over,
+        out_shape=[jax.ShapeDtypeStruct(cells, F32)] * 2,
+        in_specs=hbm,
+        out_specs=hbm,
+        scratch_shapes=[pltpu.VMEM(cells, F32), pltpu.VMEM(cells, F32), pltpu.SemaphoreType.DMA((4,))],
+        name="hand_over",
+    )(*results)
     return increment.reshape(flux.shape), gradient.reshape(flux.shape)
 
 

time: 71.7 us -> 66 us (0.921)
  other arithmetic: 2.94 us -> 0 us
  Pallas kernels: 66.7 us -> 65.2 us
  local copies, waits for them, and re-layouts: 1.34 us -> 0 us
    sub x1 -> x0, other arithmetic: 2.94 us -> none  [body(): gradient = first - alpha * product]
    pallas_call x1 -> x2, Pallas kernels: 66.7 us -> 65.2 us  [the longest x1 63.6 us: body(): pl.pallas_call(kernel, out_shape=[jax.ShapeDtypeStruct(cells, F32)] * 2,...]
    slice x1 -> x0, local copies, waits for them, and re-layouts: 1.34 us -> none  [body(): alpha, last_alpha = (alphas[0, 0], alphas[0, LANES - 1])]
where the time goes in v3:
time: 66 us; the launch traced here: 65.9 us
  Pallas kernels  65.2 us (99%)
    pallas_call x1, Pallas kernels, body(): pl.pallas_call(kernel, out_shape=[jax.ShapeDtypeStruct(cells, F32)] * 2,...  63.6 us
    pallas_call x1, Pallas kernels, body(): pl.pallas_call(hand_over, out_shape=[jax.ShapeDtypeStruct(cells, F32)] *...  1.66 us

profile of v3, /device:TPU:1, one launch (start us, length us, event | category | flops | bytes accessed | tf_op | source)
XLA Modules:
  0.0 65.9 jit_solution(5534033902182936322)
XLA Ops:
  0.6 63.6 %inversion.1 = (f32[256,128]{1,0:T(8,128)}, f32[256,128]{1,0:T(8,128)}) custom-call(f32[256,128]{1,0:T(8,128)} %bitcast.16, f32[256,128]{1,0:T(8,128)} %bitcast.17, f32[256,128]{1,0:T(8,128)} %bitcast.18, f32[128,128]{1,0:T(8,128)} %bitcast.19, f32[128,128]{1,0:T(8,128)} %bitcast.20, f32[256,4096]{1,0:T(8,128)} %bitcast.15, s32[1,32]{1,0:T(1,128)} %bitcast.23, ...), custom_call_target="tpu_custom_call" | custom-call | tf_op jit(solution)/shard_map/inversion/pallas_call | solution.py:351
  64.2 1.7 %hand_over.1 = (f32[256,128]{1,0:T(8,128)}, f32[256,128]{1,0:T(8,128)}) custom-call(f32[256,128]{1,0:T(8,128)} %get-tuple-element.6.a, f32[256,128]{1,0:T(8,128)} %get-tuple-element.7.b), custom_call_target="tpu_custom_call" | custom-call | tf_op jit(solution)/shard_map/hand_over/pallas_call | solution.py:410

commit v4 on v2

--- a/solution.py
+++ b/solution.py
@@ -79,12 +79,12 @@
 
 def kernel(
     flux_hbm, prior_hbm, precision_hbm, value_hbm, weight_hbm, foot, counts_hbm, obs_hbm, cell_hbm,
-    first_out, product_out, alphas,
+    scaled_hbm, gradient_hbm, alphas,
     flux, prior, precision, value, weight, counts, obs_blocks, cell_blocks,
-    foot_in, foot_t, picked, part, cells, prec, gap, onehot_c, onehot_a, observed,
+    foot_in, foot_t, part, cells, prec, pull, terms, found, pulled, onehot_c, meet, onehot_a, observed,
     first_fwd_out, first_fwd_in, fwd_out, fwd_in, back_out, back_in, last_back_out, last_back_in,
-    core_out, core_in, last_out, last_in,
-    foot_sem, in_sem, send_sem, recv_sem,
+    core_out, core_in, last_out, last_in, scaled, gradient,
+    foot_sem, in_sem, send_sem, recv_sem, out_sem,
 ):
     region, slot = lax.axis_index("region"), lax.axis_index("slot")
     y, core = lax.div(slot, 2), lax.rem(slot, 2)
@@ -135,17 +135,24 @@
             device_id_type=MESH,
         )
 
-    def send(exchange, source, target):
+    def send(exchange, source, target, rows=1):
         for dz, dx, dy in STEPS:
             there = at_z[dz] + at_x[dx]
+            chip = row_at[dy] + there if source.shape[0] > 1 else 0
             remote(
-                source(row_at[dy] + there), target.at[me], exchange,
+                source.at[pl.ds(chip * rows, rows), :], target.at[pl.ds(me * rows, rows), :], exchange,
                 {"region": there, "slot": slot_at[dy]},
             ).start()
 
-    def finish(exchange, target):
-        others = target.at[pl.ds(0, CHIPS - 1)]
+    def finish(exchange, target, rows=1):
+        others = target.at[pl.ds(0, (CHIPS - 1) * rows), :]
         return remote(others, others, exchange, partner)
+
+    def keep(source, target, rows=1):
+        target[pl.ds(me * rows, rows), :] = source[pl.ds(me * rows, rows), :]
+
+    def every_other(first):
+        return pl.ds(first, CHIPS, stride=2)
 
     lane = iota((REGIONS, BLOCKS), 1)
     of_region = lane % REGIONS == iota((REGIONS, BLOCKS), 0)
@@ -169,16 +176,8 @@
 
     group = iota((1, LANES), 1) // REGIONS
 
-    def pick_cells(field):
-        found = pick(field, onehot_c[...], AS_IS)
-        for k in range(MOST):
-            half = found[:, k // 4 * LANES : (k // 4 + 1) * LANES]
-            half = jnp.where(group == k % 4, half, 0.0)
-            half = half + pltpu.roll(half, 2 * REGIONS, 1)
-            picked[k] = half + pltpu.roll(half, REGIONS, 1)
-
     loads[3].wait()
-    pick_cells(load_cells(flux))
+    found[...] = pick(load_cells(flux), onehot_c[...], AS_IS)
 
     loads[0].wait()
     index = jnp.concatenate(
@@ -186,13 +185,13 @@
     )
     index = jnp.concatenate([index, jnp.zeros((LANES - MOST, LANES), F32)], axis=0).T
     index = jnp.concatenate([index[:REGIONS]] * 4, axis=0)
-    first_fwd_out[:, 1:, :] = index.reshape(CHIPS, 1, LANES)
+    first_fwd_out[every_other(1), :] = index
 
     for pair in range(PAIRS):
         for share in range(4):
             foot_copy(share * PAIRS + pair).wait()
 
-        @pl.loop(0, MOST)
+        @pl.loop(0, MOST, unroll=MOST)
         def _(k):
             block = [
                 foot_in[pl.ds((share * PAIRS + pair) * BLOCKS + k, REGIONS, stride=MOST), :]
@@ -201,16 +200,29 @@
             block = jnp.concatenate(block, axis=0).T
             foot_t[pl.ds(k * SHARE + 2 * pair, 2)] = block.reshape(2, BLOCK, LANES)
 
-    def partials():
-        @pl.loop(0, MOST)
-        def _(k):
-            field = picked[k]
-            rows = [
-                jnp.sum(foot_t[k * SHARE + i] * field, axis=0, keepdims=True) for i in range(SHARE)
-            ]
-            part[pl.ds(pl.multiple_of(k * SHARE, SHARE), SHARE), :] = jnp.concatenate(rows, axis=0)
-
-        return part[...].T.reshape(CHIPS, 1, LANES)
+    low = [iota((8, LANES), 0) // shift % 2 == 0 for shift in (1, 2, 4)]
+
+    def partials(picked):
+        rows = []
+        for k in range(MOST):
+            field = picked[:, k // 4 * LANES : (k // 4 + 1) * LANES]
+            field = jnp.where(group == k % 4, field, 0.0)
+            field = field + pltpu.roll(field, 2 * REGIONS, 1)
+            field = field + pltpu.roll(field, REGIONS, 1)
+            for start in range(0, SHARE, 8):
+                sums = []
+                for i in range(start, start + 8):
+                    acc = foot_t[k * SHARE + i, :8, :] * field[:8]
+                    for c in range(8, BLOCK, 8):
+                        acc = acc + foot_t[k * SHARE + i, c : c + 8, :] * field[c : c + 8]
+                    sums.append(acc)
+                for mask, shift in zip(low, (1, 2, 4)):
+                    sums = [
+                        jnp.where(mask, a, b) + pltpu.roll(jnp.where(mask, b, a), 8 - shift, 0)
+                        for a, b in zip(sums[::2], sums[1::2])
+                    ]
+                rows += sums
+        return jnp.concatenate(rows, axis=0).T
 
     def summed(came, step, numer, denom):
         dense = pick(side_by_side(came.T), onehot_a[...], AS_IS)
@@ -224,7 +236,7 @@
         return both[:SHARE], scalars[:, :1], scalars[:, LANES : LANES + 1]
 
     def to_sources(weighted):
-        return stacked(pick(weighted, onehot_a[...], TURNED)).T.reshape(CHIPS, 1, LANES)
+        return stacked(pick(weighted, onehot_a[...], TURNED)).T
 
     def adjoint(came):
         part[...] = came.T
@@ -241,7 +253,7 @@
                 acc = acc + pltpu.roll(acc, REGIONS, 1)
                 merged = jnp.where(group == place, acc, merged)
             halves.append(merged)
-        return pick(jnp.concatenate(halves, axis=1), onehot_c[...], TURNED)
+        return jnp.concatenate(halves, axis=1)
 
     left = iota((1, LANES), 1) < LANES // 2
 
@@ -249,81 +261,115 @@
         scalars = jnp.sum(rows, axis=0, keepdims=True)
         return scalars[:, :1] / scalars[:, LANES // 2 : LANES // 2 + 1]
 
-    first_fwd_out[:, :1, :] = partials()
-    first_fwd_in[me] = first_fwd_out[me]
+    first_fwd_out[every_other(0), :] = partials(found[...])
+    keep(first_fwd_out, first_fwd_in, 2)
     pl.semaphore_wait(barrier, CHIPS)
-    send(FWD[0], lambda chip: first_fwd_out.at[chip], first_fwd_in)
+    send(FWD[0], first_fwd_out, first_fwd_in, 2)
     for load in loads[4:]:
         load.wait()
-    gap[...] = load_cells(flux) - load_cells(prior)
     prec[...] = load_cells(precision)
+    pull[...] = prec[...] * (load_cells(flux) - load_cells(prior))
+    pulled[...] = pick(pull[...], onehot_c[...], AS_IS)
+    meet[...] = lax.dot_general(
+        onehot_c[...], onehot_c[...], (((0,), (0,)), ((), ())), preferred_element_type=F32
+    ).astype(BF16)
     observed[0] = value[...].T.reshape(2, BLOCK, LANES)
     observed[1] = weight[...].T.reshape(2, BLOCK, LANES)
     mine = pl.ds(pl.multiple_of(y * SHARE, SHARE), SHARE)
     seen = jnp.concatenate([observed[0, 0, mine, :], observed[0, 1, mine, :]], axis=1)
     weights = jnp.concatenate([observed[1, 0, mine, :], observed[1, 1, mine, :]], axis=1)
-    finish(FWD[0], first_fwd_in).wait_recv()
-    index = first_fwd_in[:, 1, :]
+    finish(FWD[0], first_fwd_in, 2).wait_recv()
+    index = first_fwd_in[every_other(1), :]
     column = iota((LANES, OBLK), 1)
     block = ((column % LANES) * 2 + column // LANES).astype(F32)
     for k in range(MOST):
         onehot_a[k * LANES : (k + 1) * LANES, :] = jnp.where(
             index[:, k : k + 1] == block, 1.0, 0.0
         ).astype(BF16)
-    image, _, _ = summed(first_fwd_in[:, 0, :], 0, 0.0, 0.0)
+    image, _, _ = summed(first_fwd_in[every_other(0), :], 0, 0.0, 0.0)
     back_out[...] = to_sources(weights * (image - seen))
-    back_in[me] = back_out[me]
-    send(BACK[0], lambda chip: back_out.at[chip], back_in)
+    keep(back_out, back_in)
+    send(BACK[0], back_out, back_in)
     finish(BACK[0], back_in).wait_recv()
-    first = adjoint(back_in[...].reshape(CHIPS, LANES)) + prec[...] * gap[...]
+
+    term = adjoint(back_in[...])
+    terms[...] = term
+    picked = pick(term, meet[...], AS_IS) + pulled[...]
+    found[...] = picked
+    fwd_out[0] = partials(picked)
+    keep(fwd_out.at[0], fwd_in.at[0])
+    send(FWD[1], fwd_out.at[0], fwd_in.at[0])
+    first = pick(terms[...], onehot_c[...], TURNED) + pull[...]
     cells[...] = first
-
-    pick_cells(first)
-    fwd_out[0] = partials()
-    fwd_in[0, me] = fwd_out[0, me]
-    send(FWD[1], lambda chip: fwd_out.at[0, chip], fwd_in.at[0])
-    first = cells[...]
-    first_out[...] = store_cells(first)
+    pulled[...] = pick(prec[...] * first, onehot_c[...], AS_IS)
+    scaled[...] = store_cells(first)
     square = first * first
     numer, denom = total(square), total(prec[...] * square)
     finish(FWD[1], fwd_in.at[0]).wait_recv()
-    image, numer, denom = summed(fwd_in[0].reshape(CHIPS, LANES), 1, numer, denom)
+    image, numer, denom = summed(fwd_in[0], 1, numer, denom)
     weighted = weights * image
-    last_back_out[:, :1, :] = to_sources(weighted)
+    last_back_out[every_other(0), :] = to_sources(weighted)
     scalars = jnp.where(left, numer, denom + total(weighted * image))
-    last_back_out[:, 1:, :] = jnp.broadcast_to(scalars.reshape(1, 1, LANES), (CHIPS, 1, LANES))
-    last_back_in[me] = last_back_out[me]
-    send(BACK[1], lambda chip: last_back_out.at[chip], last_back_in)
-    finish(BACK[1], last_back_in).wait_recv()
+    last_back_out[every_other(1), :] = jnp.broadcast_to(scalars, (CHIPS, LANES))
+    keep(last_back_out, last_back_in, 2)
+    send(BACK[1], last_back_out, last_back_in, 2)
+    finish(BACK[1], last_back_in, 2).wait_recv()
+    alpha = ratio(last_back_in[every_other(1), :])
+
+    term = adjoint(last_back_in[every_other(0), :])
+    terms[...] = term
+    picked = found[...] - alpha * (pick(term, meet[...], AS_IS) + pulled[...])
+    fwd_out[1] = partials(picked)
+    keep(fwd_out.at[1], fwd_in.at[1])
+    send(FWD[2], fwd_out.at[1], fwd_in.at[1])
     first = cells[...]
-    product = adjoint(last_back_in[:, 0, :]) + prec[...] * first
-    alpha = ratio(last_back_in[:, 1, :])
-
-    second = first - alpha * product
-    cells[...] = second
-    pick_cells(second)
-    fwd_out[1] = partials()
-    fwd_in[1, me] = fwd_out[1, me]
-    send(FWD[2], lambda chip: fwd_out.at[1, chip], fwd_in.at[1])
-    product_out[...] = store_cells(product)
-    second = cells[...]
+    second = first - alpha * (pick(terms[...], onehot_c[...], TURNED) + prec[...] * first)
+    gradient[...] = store_cells(second)
+    scaled[...] = scaled[...] * alpha
+    results = [
+        pltpu.make_async_copy(gradient, gradient_hbm, out_sem.at[0]),
+        pltpu.make_async_copy(scaled, scaled_hbm, out_sem.at[1]),
+    ]
+    for result in results:
+        result.start()
     square = second * second
     numer, denom = total(square), total(prec[...] * square)
     finish(FWD[2], fwd_in.at[1]).wait_recv()
-    image, numer, denom = summed(fwd_in[1].reshape(CHIPS, LANES), 2, numer, denom)
+    image, numer, denom = summed(fwd_in[1], 2, numer, denom)
     last_out[...] = jnp.where(left, numer, denom + total(weights * image * image))
-    last_in[me] = last_out[...]
-    send(LAST, lambda chip: last_out, last_in)
+    last_in[pl.ds(me, 1), :] = last_out[...]
+    send(LAST, last_out, last_in)
     finish(LAST, last_in).wait_recv()
-    alphas[...] = jnp.where(left, alpha, ratio(last_in[...].reshape(CHIPS, LANES)))
-
-    for exchange, target in (
-        (FWD[0], first_fwd_in), (BACK[0], back_in), (FWD[1], fwd_in.at[0]),
-        (BACK[1], last_back_in), (FWD[2], fwd_in.at[1]), (LAST, last_in),
+    alphas[...] = jnp.broadcast_to(ratio(last_in[...]), (1, LANES))
+    for result in results:
+        result.wait()
+
+    for exchange, target, rows in (
+        (FWD[0], first_fwd_in, 2), (BACK[0], back_in, 1), (FWD[1], fwd_in.at[0], 1),
+        (BACK[1], last_back_in, 2), (FWD[2], fwd_in.at[1], 1), (LAST, last_in, 1),
     ):
-        finish(exchange, target).wait_send()
+        finish(exchange, target, rows).wait_send()
     for step in range(3):
         remote(core_out.at[step], core_in.at[step], CORE[step], partner).wait_send()
+
+
+def finish_step(scaled, gradient, alphas, increment_out, gradient_out, a, b, c, d, sem):
+    copies = [
+        pltpu.make_async_copy(source, target, sem.at[i])
+        for i, (source, target) in enumerate(
+            ((alphas, c), (gradient, b), (scaled, a), (b, gradient_out), (d, increment_out))
+        )
+    ]
+    for copy in copies[:3]:
+        copy.start()
+    copies[1].wait()
+    copies[3].start()
+    copies[0].wait()
+    copies[2].wait()
+    d[...] = -(a[...] + c[...] * b[...])
+    copies[4].start()
+    copies[3].wait()
+    copies[4].wait()
 
 
 def body(
@@ -331,16 +377,12 @@
     cell_blocks,
 ):
     cells = (256, LANES)
-    message, double = (CHIPS, 1, LANES), (CHIPS, 2, LANES)
-    first, product, alphas = pl.pallas_call(
+    message, double = (CHIPS, LANES), (2 * CHIPS, LANES)
+    results = pl.pallas_call(
         kernel,
-        out_shape=[
-            jax.ShapeDtypeStruct(cells, F32),
-            jax.ShapeDtypeStruct(cells, F32),
-            jax.ShapeDtypeStruct((1, LANES), F32),
-        ],
+        out_shape=[jax.ShapeDtypeStruct(cells, F32)] * 2 + [jax.ShapeDtypeStruct((1, LANES), F32)],
         in_specs=[pl.BlockSpec(memory_space=pltpu.HBM)] * 9,
-        out_specs=[pl.BlockSpec(memory_space=pltpu.VMEM)] * 3,
+        out_specs=[pl.BlockSpec(memory_space=pltpu.HBM)] * 2 + [pl.BlockSpec(memory_space=pltpu.VMEM)],
         scratch_shapes=[
             pltpu.VMEM(cells, F32),
             pltpu.VMEM(cells, F32),
@@ -352,12 +394,15 @@
             pltpu.VMEM((MOST, REGIONS), jnp.int32),
             pltpu.VMEM((TILES * BLOCKS, LANES), F32),
             pltpu.VMEM((MOST * SHARE, BLOCK, LANES), F32),
-            pltpu.VMEM((MOST, BLOCK, LANES), F32),
             pltpu.VMEM((LANES, LANES), F32),
             pltpu.VMEM((BLOCK, CBLK), F32),
             pltpu.VMEM((BLOCK, CBLK), F32),
             pltpu.VMEM((BLOCK, CBLK), F32),
+            pltpu.VMEM((BLOCK, BLOCKS), F32),
+            pltpu.VMEM((BLOCK, BLOCKS), F32),
+            pltpu.VMEM((BLOCK, BLOCKS), F32),
             pltpu.VMEM((CBLK, BLOCKS), BF16),
+            pltpu.VMEM((BLOCKS, BLOCKS), BF16),
             pltpu.VMEM((MOST * LANES, OBLK), BF16),
             pltpu.VMEM((2, 2, BLOCK, LANES), F32),
             pltpu.VMEM(double, F32),
@@ -372,10 +417,13 @@
             pltpu.VMEM((3, SHARE + 8, OBLK), F32),
             pltpu.VMEM((1, LANES), F32),
             pltpu.VMEM(message, F32),
+            pltpu.VMEM(cells, F32),
+            pltpu.VMEM(cells, F32),
             pltpu.SemaphoreType.DMA((TILES,)),
             pltpu.SemaphoreType.DMA((8,)),
             pltpu.SemaphoreType.DMA((EXCHANGES,)),
             pltpu.SemaphoreType.DMA((EXCHANGES,)),
+            pltpu.SemaphoreType.DMA((2,)),
         ],
         compiler_params=pltpu.CompilerParams(
             collective_id=0, has_side_effects=True, vmem_limit_bytes=60 * 1024 * 1024
@@ -392,9 +440,21 @@
         obs_blocks.reshape(REGIONS, MOST).T,
         cell_blocks.reshape(REGIONS, MOST).T,
     )
-    alpha, last_alpha = alphas[0, 0], alphas[0, LANES - 1]
-    gradient = first - alpha * product
-    increment = -(alpha * first + last_alpha * gradient)
+    hbm = [pl.BlockSpec(memory_space=pltpu.HBM)]
+    increment, gradient = pl.pallas_call(
+        finish_step,
+        out_shape=[jax.ShapeDtypeStruct(cells, F32)] * 2,
+        in_specs=hbm * 3,
+        out_specs=hbm * 2,
+        scratch_shapes=[
+            pltpu.VMEM(cells, F32),
+            pltpu.VMEM(cells, F32),
+            pltpu.VMEM((1, LANES), F32),
+            pltpu.VMEM(cells, F32),
+            pltpu.SemaphoreType.DMA((5,)),
+        ],
+        name="finish_step",
+    )(*results)
     return increment.reshape(flux.shape), gradient.reshape(flux.shape)
 
 

time: 71.7 us -> 64.1 us (0.89)
  Pallas kernels: 66.7 us -> 63.3 us
  other arithmetic: 2.94 us -> 0 us
  local copies, waits for them, and re-layouts: 1.34 us -> 0 us
    pallas_call x1 -> x2, Pallas kernels: 66.7 us -> 63.3 us  [the longest x1 61.6 us: body(): pl.pallas_call(kernel, out_shape=[jax.ShapeDtypeStruct(cells, F32)] * 2 +...]
    sub x1 -> x0, other arithmetic: 2.94 us -> none  [body(): gradient = first - alpha * product]
    slice x1 -> x0, local copies, waits for them, and re-layouts: 1.34 us -> none  [body(): alpha, last_alpha = (alphas[0, 0], alphas[0, LANES - 1])]
where the time goes in v4:
time: 64.1 us; the launch traced here: 64 us
  Pallas kernels  63.3 us (99%)
    pallas_call x1, Pallas kernels, body(): pl.pallas_call(kernel, out_shape=[jax.ShapeDtypeStruct(cells, F32)] * 2 +...  61.6 us
    pallas_call x1, Pallas kernels, body(): pl.pallas_call(finish_step, out_shape=[jax.ShapeDtypeStruct(cells, F32)]...  1.69 us

profile of v4, /device:TPU:1, one launch (start us, length us, event | category | flops | bytes accessed | tf_op | source)
XLA Modules:
  0.0 64.0 jit_solution(10549288978736136451)
XLA Ops:
  0.6 61.6 %inversion.1 = (f32[256,128]{1,0:T(8,128)}, f32[256,128]{1,0:T(8,128)}, f32[1,128]{1,0:T(1,128)}) custom-call(f32[256,128]{1,0:T(8,128)} %bitcast.16, f32[256,128]{1,0:T(8,128)} %bitcast.17, f32[256,128]{1,0:T(8,128)} %bitcast.18, f32[128,128]{1,0:T(8,128)} %bitcast.19, f32[128,128]{1,0:T(8,128)} %bitcast.20, f32[256,4096]{1,0:T(8,128)} %bitcast.15, ...), custom_call_target="tpu_custom_call" | custom-call | tf_op jit(solution)/shard_map/inversion/pallas_call | solution.py:381
  62.3 1.7 %finish_step.1 = (f32[256,128]{1,0:T(8,128)}, f32[256,128]{1,0:T(8,128)}) custom-call(f32[256,128]{1,0:T(8,128)} %get-tuple-element.7.scaled, f32[256,128]{1,0:T(8,128)} %get-tuple-element.8.gradient, f32[1,128]{1,0:T(1,128)} %get-tuple-element.9.alphas), custom_call_target="tpu_custom_call" | custom-call | tf_op jit(solution)/shard_map/finish_step/pallas_call | solution.py:444

commit v5 on v4

--- a/solution.py
+++ b/solution.py
@@ -23,8 +23,8 @@
 AS_IS = ((1,), (0,))
 TURNED = ((1,), (1,))
 
-FWD, BACK, LAST, CORE = (0, 1, 2), (3, 4), 5, (6, 7, 8)
-EXCHANGES = 9
+FWD, BACK, LAST, CORE, SUMS = (0, 1, 2), (3, 4), 5, (6, 7, 8), 9
+EXCHANGES = 10
 
 
 def hops(step):
@@ -83,7 +83,7 @@
     flux, prior, precision, value, weight, counts, obs_blocks, cell_blocks,
     foot_in, foot_t, part, cells, prec, pull, terms, found, pulled, onehot_c, meet, onehot_a, observed,
     first_fwd_out, first_fwd_in, fwd_out, fwd_in, back_out, back_in, last_back_out, last_back_in,
-    core_out, core_in, last_out, last_in, scaled, gradient,
+    core_out, core_in, first_image, sum_out, sum_in, last_out, last_in, scaled, gradient,
     foot_sem, in_sem, send_sem, recv_sem, out_sem,
 ):
     region, slot = lax.axis_index("region"), lax.axis_index("slot")
@@ -295,7 +295,6 @@
     term = adjoint(back_in[...])
     terms[...] = term
     picked = pick(term, meet[...], AS_IS) + pulled[...]
-    found[...] = picked
     fwd_out[0] = partials(picked)
     keep(fwd_out.at[0], fwd_in.at[0])
     send(FWD[1], fwd_out.at[0], fwd_in.at[0])
@@ -307,21 +306,24 @@
     numer, denom = total(square), total(prec[...] * square)
     finish(FWD[1], fwd_in.at[0]).wait_recv()
     image, numer, denom = summed(fwd_in[0], 1, numer, denom)
+    first_image[...] = image
     weighted = weights * image
-    last_back_out[every_other(0), :] = to_sources(weighted)
-    scalars = jnp.where(left, numer, denom + total(weighted * image))
-    last_back_out[every_other(1), :] = jnp.broadcast_to(scalars, (CHIPS, LANES))
-    keep(last_back_out, last_back_in, 2)
-    send(BACK[1], last_back_out, last_back_in, 2)
-    finish(BACK[1], last_back_in, 2).wait_recv()
-    alpha = ratio(last_back_in[every_other(1), :])
-
-    term = adjoint(last_back_in[every_other(0), :])
+    last_back_out[...] = to_sources(weighted)
+    keep(last_back_out, last_back_in)
+    send(BACK[1], last_back_out, last_back_in)
+    sum_out[...] = jnp.where(left, numer, denom + total(weighted * image))
+    sum_in[pl.ds(me, 1), :] = sum_out[...]
+    send(SUMS, sum_out, sum_in)
+    finish(BACK[1], last_back_in).wait_recv()
+
+    term = adjoint(last_back_in[...])
     terms[...] = term
-    picked = found[...] - alpha * (pick(term, meet[...], AS_IS) + pulled[...])
+    picked = pick(term, meet[...], AS_IS) + pulled[...]
     fwd_out[1] = partials(picked)
     keep(fwd_out.at[1], fwd_in.at[1])
     send(FWD[2], fwd_out.at[1], fwd_in.at[1])
+    finish(SUMS, sum_in).wait_recv()
+    alpha = ratio(sum_in[...])
     first = cells[...]
     second = first - alpha * (pick(terms[...], onehot_c[...], TURNED) + prec[...] * first)
     gradient[...] = store_cells(second)
@@ -336,6 +338,7 @@
     numer, denom = total(square), total(prec[...] * square)
     finish(FWD[2], fwd_in.at[1]).wait_recv()
     image, numer, denom = summed(fwd_in[1], 2, numer, denom)
+    image = first_image[...] - alpha * image
     last_out[...] = jnp.where(left, numer, denom + total(weights * image * image))
     last_in[pl.ds(me, 1), :] = last_out[...]
     send(LAST, last_out, last_in)
@@ -346,7 +349,7 @@
 
     for exchange, target, rows in (
         (FWD[0], first_fwd_in, 2), (BACK[0], back_in, 1), (FWD[1], fwd_in.at[0], 1),
-        (BACK[1], last_back_in, 2), (FWD[2], fwd_in.at[1], 1), (LAST, last_in, 1),
+        (BACK[1], last_back_in, 1), (FWD[2], fwd_in.at[1], 1), (LAST, last_in, 1), (SUMS, sum_in, 1),
     ):
         finish(exchange, target, rows).wait_send()
     for step in range(3):
@@ -411,10 +414,13 @@
             pltpu.VMEM((2, *message), F32),
             pltpu.VMEM(message, F32),
             pltpu.VMEM(message, F32),
-            pltpu.VMEM(double, F32),
-            pltpu.VMEM(double, F32),
+            pltpu.VMEM(message, F32),
+            pltpu.VMEM(message, F32),
             pltpu.VMEM((3, SHARE + 8, OBLK), F32),
             pltpu.VMEM((3, SHARE + 8, OBLK), F32),
+            pltpu.VMEM((SHARE, OBLK), F32),
+            pltpu.VMEM((1, LANES), F32),
+            pltpu.VMEM(message, F32),
             pltpu.VMEM((1, LANES), F32),
             pltpu.VMEM(message, F32),
             pltpu.VMEM(cells, F32),

time: 64.1 us -> 64 us (level)
  no operation moved by 1% of the time
where the time goes in v5:
time: 64 us; the launch traced here: 63.9 us
  Pallas kernels  63.3 us (99%)
  between operations  0.64 us (1%)
    pallas_call x1, Pallas kernels, body(): pl.pallas_call(kernel, out_shape=[jax.ShapeDtypeStruct(cells, F32)] * 2 +...  61.6 us
    pallas_call x1, Pallas kernels, body(): pl.pallas_call(finish_step, out_shape=[jax.ShapeDtypeStruct(cells, F32)]...  1.69 us

profile of v5, /device:TPU:1, one launch (start us, length us, event | category | flops | bytes accessed | tf_op | source)
XLA Modules:
  0.0 63.9 jit_solution(15197798637073015549)
XLA Ops:
  0.6 61.6 %inversion.1 = (f32[256,128]{1,0:T(8,128)}, f32[256,128]{1,0:T(8,128)}, f32[1,128]{1,0:T(1,128)}) custom-call(f32[256,128]{1,0:T(8,128)} %bitcast.16, f32[256,128]{1,0:T(8,128)} %bitcast.17, f32[256,128]{1,0:T(8,128)} %bitcast.18, f32[128,128]{1,0:T(8,128)} %bitcast.19, f32[128,128]{1,0:T(8,128)} %bitcast.20, f32[256,4096]{1,0:T(8,128)} %bitcast.15, ...), custom_call_target="tpu_custom_call" | custom-call | tf_op jit(solution)/shard_map/inversion/pallas_call | solution.py:384
  62.2 1.7 %finish_step.1 = (f32[256,128]{1,0:T(8,128)}, f32[256,128]{1,0:T(8,128)}) custom-call(f32[256,128]{1,0:T(8,128)} %get-tuple-element.7.scaled, f32[256,128]{1,0:T(8,128)} %get-tuple-element.8.gradient, f32[1,128]{1,0:T(1,128)} %get-tuple-element.9.alphas), custom_call_target="tpu_custom_call" | custom-call | tf_op jit(solution)/shard_map/finish_step/pallas_call | solution.py:450

commit v6 on v5

--- a/solution.py
+++ b/solution.py
@@ -23,8 +23,8 @@
 AS_IS = ((1,), (0,))
 TURNED = ((1,), (1,))
 
-FWD, BACK, LAST, CORE, SUMS = (0, 1, 2), (3, 4), 5, (6, 7, 8), 9
-EXCHANGES = 10
+FWD, BACK, LAST, CORE, PLANE, LINE = (0, 1, 2), (3, 4), 5, (6, 7, 8), 9, 10
+EXCHANGES = 11
 
 
 def hops(step):
@@ -83,7 +83,7 @@
     flux, prior, precision, value, weight, counts, obs_blocks, cell_blocks,
     foot_in, foot_t, part, cells, prec, pull, terms, found, pulled, onehot_c, meet, onehot_a, observed,
     first_fwd_out, first_fwd_in, fwd_out, fwd_in, back_out, back_in, last_back_out, last_back_in,
-    core_out, core_in, first_image, sum_out, sum_in, last_out, last_in, scaled, gradient,
+    core_out, core_in, first_image, plane_out, plane_in, line_out, line_in, last_out, last_in, scaled, gradient,
     foot_sem, in_sem, send_sem, recv_sem, out_sem,
 ):
     region, slot = lax.axis_index("region"), lax.axis_index("slot")
@@ -144,8 +144,8 @@
                 {"region": there, "slot": slot_at[dy]},
             ).start()
 
-    def finish(exchange, target, rows=1):
-        others = target.at[pl.ds(0, (CHIPS - 1) * rows), :]
+    def finish(exchange, target, rows=1, count=CHIPS - 1):
+        others = target.at[pl.ds(0, count * rows), :]
         return remote(others, others, exchange, partner)
 
     def keep(source, target, rows=1):
@@ -311,9 +311,14 @@
     last_back_out[...] = to_sources(weighted)
     keep(last_back_out, last_back_in)
     send(BACK[1], last_back_out, last_back_in)
-    sum_out[...] = jnp.where(left, numer, denom + total(weighted * image))
-    sum_in[pl.ds(me, 1), :] = sum_out[...]
-    send(SUMS, sum_out, sum_in)
+    plane_out[...] = jnp.where(left, numer, denom + total(weighted * image))
+    plane_in[pl.ds(y * 4 + x, 1), :] = plane_out[...]
+    for dz, dx, dy in STEPS:
+        if dz == 0:
+            remote(
+                plane_out, plane_in.at[pl.ds(y * 4 + x, 1), :], PLANE,
+                {"region": at_z[0] + at_x[dx], "slot": slot_at[dy]},
+            ).start()
     finish(BACK[1], last_back_in).wait_recv()
 
     term = adjoint(last_back_in[...])
@@ -322,8 +327,15 @@
     fwd_out[1] = partials(picked)
     keep(fwd_out.at[1], fwd_in.at[1])
     send(FWD[2], fwd_out.at[1], fwd_in.at[1])
-    finish(SUMS, sum_in).wait_recv()
-    alpha = ratio(sum_in[...])
+    finish(PLANE, plane_in, count=15).wait_recv()
+    line_out[...] = jnp.sum(plane_in[...], axis=0, keepdims=True)
+    line_in[pl.ds(z, 1), :] = line_out[...]
+    for dz in (4, 3, 5, 2, 6, 1, 7):
+        remote(
+            line_out, line_in.at[pl.ds(z, 1), :], LINE, {"region": at_z[dz] + at_x[0], "slot": slot}
+        ).start()
+    finish(LINE, line_in, count=7).wait_recv()
+    alpha = ratio(line_in[...])
     first = cells[...]
     second = first - alpha * (pick(terms[...], onehot_c[...], TURNED) + prec[...] * first)
     gradient[...] = store_cells(second)
@@ -349,9 +361,11 @@
 
     for exchange, target, rows in (
         (FWD[0], first_fwd_in, 2), (BACK[0], back_in, 1), (FWD[1], fwd_in.at[0], 1),
-        (BACK[1], last_back_in, 1), (FWD[2], fwd_in.at[1], 1), (LAST, last_in, 1), (SUMS, sum_in, 1),
+        (BACK[1], last_back_in, 1), (FWD[2], fwd_in.at[1], 1), (LAST, last_in, 1),
     ):
         finish(exchange, target, rows).wait_send()
+    finish(PLANE, plane_in, count=15).wait_send()
+    finish(LINE, line_in, count=7).wait_send()
     for step in range(3):
         remote(core_out.at[step], core_in.at[step], CORE[step], partner).wait_send()
 
@@ -420,7 +434,9 @@
             pltpu.VMEM((3, SHARE + 8, OBLK), F32),
             pltpu.VMEM((SHARE, OBLK), F32),
             pltpu.VMEM((1, LANES), F32),
-            pltpu.VMEM(message, F32),
+            pltpu.VMEM((16, LANES), F32),
+            pltpu.VMEM((1, LANES), F32),
+            pltpu.VMEM((8, LANES), F32),
             pltpu.VMEM((1, LANES), F32),
             pltpu.VMEM(message, F32),
             pltpu.VMEM(cells, F32),

time: 64 us -> 64 us (level)
  no operation moved by 1% of the time
where the time goes in v6:
time: 64 us; the launch traced here: 63.9 us
  Pallas kernels  63.2 us (99%)
  between operations  0.64 us (1%)
    pallas_call x1, Pallas kernels, body(): pl.pallas_call(kernel, out_shape=[jax.ShapeDtypeStruct(cells, F32)] * 2 +...  61.5 us
    pallas_call x1, Pallas kernels, body(): pl.pallas_call(finish_step, out_shape=[jax.ShapeDtypeStruct(cells, F32)]...  1.69 us

profile of v6, /device:TPU:1, one launch (start us, length us, event | category | flops | bytes accessed | tf_op | source)
XLA Modules:
  0.0 63.9 jit_solution(16463343079079434892)
XLA Ops:
  0.6 61.5 %inversion.1 = (f32[256,128]{1,0:T(8,128)}, f32[256,128]{1,0:T(8,128)}, f32[1,128]{1,0:T(1,128)}) custom-call(f32[256,128]{1,0:T(8,128)} %bitcast.16, f32[256,128]{1,0:T(8,128)} %bitcast.17, f32[256,128]{1,0:T(8,128)} %bitcast.18, f32[128,128]{1,0:T(8,128)} %bitcast.19, f32[128,128]{1,0:T(8,128)} %bitcast.20, f32[256,4096]{1,0:T(8,128)} %bitcast.15, ...), custom_call_target="tpu_custom_call" | custom-call | tf_op jit(solution)/shard_map/inversion/pallas_call | solution.py:398
  62.2 1.7 %finish_step.1 = (f32[256,128]{1,0:T(8,128)}, f32[256,128]{1,0:T(8,128)}) custom-call(f32[256,128]{1,0:T(8,128)} %get-tuple-element.7.scaled, f32[256,128]{1,0:T(8,128)} %get-tuple-element.8.gradient, f32[1,128]{1,0:T(1,128)} %get-tuple-element.9.alphas), custom_call_target="tpu_custom_call" | custom-call | tf_op jit(solution)/shard_map/finish_step/pallas_call | solution.py:466
